TPU v7x, 512 devices: a whole 4x8x8 slice. The times are simulated.
512 devices in a mesh: blk: 128 (over z, y, core), dp: 4 (over x).
Axes of the slice: x: 4, y: 8, z: 8, core: 2. Of those that a mesh axis runs over, the one named last changes fastest.
Arguments:
- features: bfloat16 [4, 32768, 128], P('dp', 'blk'), may hold values from -6 to 6
- kernel_map: int32 [4, 27, 32768], P('dp', None, 'blk'), may hold values from -1 to 128, as said below
- block_counts: int32 [4, 128], P('dp'), may hold values from 128 to 256, as said below
- send_position: int32 [4, 32768], P('dp', 'blk'), may hold values from 0 to 511, as said below
- cell_source: int32 [4, 65536], P('dp', 'blk'), may hold values from 0 to 511, as said below
- conv_weight: bfloat16 [27, 128, 128], replicated, may hold values from -0.109375 to 0.109375
- down_weight: bfloat16 [1024, 256], replicated, may hold values from -0.1875 to 0.1875
- cotangent: bfloat16 [4, 8192, 256], P('dp', 'blk'), may hold values from -0.023925781 to 0.023925781
Outputs:
- coarse: bfloat16 [4, 8192, 256], P('dp', 'blk')
- grad_conv: float32 [27, 128, 128], replicated
- grad_down: float32 [1024, 256], replicated
Inputs may be any that keep to these rules, and one draw needn't show every extreme that they name: `kernel_map`: where an entry is not -1, row g + entry - 64 lies within the same scene; offset 27 // 2 has the entry 64 for every row. `block_counts`: every scene has a block with all 256 rows occupied. `send_position`: within one block's rows the entries are distinct, and no owner (entry // 4) is named by more than 4 of them; some owner is named exactly 4 times in every block. `cell_source`: the entries of one owner's 8 * 64 positions are a permutation.
All inputs are finite; a program needn't handle non-finite values.
Results may differ from a plain program's by a relative error of at most 0.005.
Values may be sent and summed in bfloat16 or wider, within the bound.
A program may use at most 64 MiB of HBM per device.

v0:
```python
import jax
import jax.numpy as jnp
from jax import lax
from jax.sharding import PartitionSpec as P

OCT = 8
HALO = 64


def with_halo(block, sides, width):
    for axis, dim in sides:
        count = lax.axis_size(axis)
        forward = [(i, i + 1) for i in range(count - 1)]
        backward = [(target, source) for source, target in forward]
        low = lax.ppermute(
            lax.slice_in_dim(block, block.shape[dim] - width, None, axis=dim), axis, forward
        )
        high = lax.ppermute(lax.slice_in_dim(block, 0, width, axis=dim), axis, backward)
        block = jnp.concatenate([low, block, high], axis=dim)
    return block


def silu_grad(pre):
    sig = jax.nn.sigmoid(pre)
    return sig * (1.0 + pre * (1.0 - sig))


def body(
    features,
    kernel_map,
    block_counts,
    send_position,
    cell_source,
    conv_weight,
    down_weight,
    cotangent,
):
    rows = features.shape[1]
    width = features.shape[2]
    block = lax.axis_index("blk")
    blocks = lax.axis_size("blk")
    counted = block_counts[0][block]
    inside = jnp.arange(rows, dtype=jnp.int32)
    live = (inside < counted // 2) | (inside >= rows - (counted - counted // 2))
    masked = jnp.where(live[:, None], features[0], jnp.zeros((), jnp.bfloat16))
    padded = with_halo(masked, (("blk", 0),), HALO)
    margin = HALO
    table = jnp.concatenate([padded, jnp.zeros((1, width), jnp.bfloat16)], 0)
    own_rows = jnp.arange(rows, dtype=jnp.int32)[None, :]
    local = jnp.where(kernel_map[0] >= 0, own_rows + kernel_map[0] - HALO + margin, padded.shape[0])

    def forward_step(total, pair):
        index_row, weight = pair
        picked = jnp.take(table, index_row, axis=0)
        return (total + jnp.dot(picked, weight, preferred_element_type=jnp.float32), None)

    pre, _ = lax.scan(forward_step, jnp.zeros((rows, width), jnp.float32), (local, conv_weight))
    hidden = (jax.nn.silu(pre) * live[:, None]).astype(jnp.bfloat16)
    position = send_position[0]
    outgoing = (
        jnp.zeros((2 * rows, width), jnp.bfloat16)
        .at[position]
        .set(hidden)
        .reshape(blocks, -1, width)
    )
    incoming = lax.all_to_all(outgoing, "blk", split_axis=0, concat_axis=0, tiled=True).reshape(
        2 * rows, width
    )
    grid = jnp.take(incoming, cell_source[0], axis=0).reshape(-1, OCT * width)
    coarse = jnp.dot(grid, down_weight, preferred_element_type=jnp.float32).astype(jnp.bfloat16)
    grad_down = lax.dot_general(
        grid, cotangent[0], (((0,), (0,)), ((), ())), preferred_element_type=jnp.float32
    )
    grad_grid = lax.dot_general(
        cotangent[0], down_weight, (((1,), (1,)), ((), ())), preferred_element_type=jnp.float32
    ).astype(jnp.bfloat16)
    returned = (
        jnp.zeros((2 * rows, width), jnp.bfloat16)
        .at[cell_source[0]]
        .set(grad_grid.reshape(-1, width))
        .reshape(blocks, -1, width)
    )
    backward = lax.all_to_all(returned, "blk", split_axis=0, concat_axis=0, tiled=True).reshape(
        2 * rows, width
    )
    grad_hidden = jnp.take(backward, position, axis=0)
    grad_pre = (grad_hidden.astype(jnp.float32) * silu_grad(pre) * live[:, None]).astype(
        jnp.bfloat16
    )

    def backward_step(carry, index_row):
        picked = jnp.take(table, index_row, axis=0)
        return (
            carry,
            lax.dot_general(
                picked, grad_pre, (((0,), (0,)), ((), ())), preferred_element_type=jnp.float32
            ),
        )

    _, grad_conv = lax.scan(backward_step, jnp.zeros((), jnp.float32), local)
    grad_conv, grad_down = lax.psum((grad_conv, grad_down), ("blk", "dp"))
    return (coarse[None], grad_conv, grad_down)


def solution(mesh):
    in_specs = (
        P("dp", "blk", None),
        P("dp", None, "blk"),
        P("dp", None),
        P("dp", "blk"),
        P("dp", "blk"),
        P(),
        P(),
        P("dp", "blk", None),
    )
    out_specs = (P("dp", "blk", None), P(), P())
    return jax.shard_map(body, mesh=mesh, in_specs=in_specs, out_specs=out_specs, check_vma=False)
```

profile of v0, /device:TPU:1, one launch (start us, length us, event | category | flops | bytes accessed | tf_op | source)
XLA Modules:
  0.0 458.6 jit_solution(14658741894196614114)
XLA Ops:
  7.2 1.3 constant_dynamic-slice_fusion.2
  11.7 0.9 bitcast_select_fusion.3
  12.7 4.6 %collective-permute-start = (bf16[64,128]{1,0:T(8,128)(2,1)S(1)}, bf16[64,128]{1,0:T(8,128)(2,1)S(1)}, u32[]{:S(2)}, u32[]{:S(2)}) collective-permute-start(bf16[64,128]{1,0:T(8,128)(2,1)S(1)} %get-tuple-element.102), channel_id=1, source_target_pairs={{0,4},{4,8},{8,12},{12,16},{16,20},{20,24},{24,28},{28,32},{32,36}... | collective-permute-start | bytes 49160 | tf_op jit(solution)/shard_map/ppermute | solution.py:15
  17.3 5.5 %collective-permute-start.1 = (bf16[64,128]{1,0:T(8,128)(2,1)S(1)}, bf16[64,128]{1,0:T(8,128)(2,1)S(1)}, u32[]{:S(2)}, u32[]{:S(2)}) collective-permute-start(bf16[64,128]{1,0:T(8,128)(2,1)S(1)} %get-tuple-element.103), channel_id=1, source_target_pairs={{4,0},{8,4},{12,8},{16,12},{20,16},{24,20},{28,24},{32,28},{36,32}... | collective-permute-start | bytes 49160 | tf_op jit(solution)/shard_map/ppermute | solution.py:18
  23.5 1.0 convolution_convert_fusion
  24.6 2.4 scatter_custom_fusion.1
  26.9 15.1 %all-to-all-start.1 = ((bf16[128,4,128]{2,1,0:T(4,128)(2,1)}), bf16[128,4,128]{2,1,0:T(4,128)(2,1)S(1)}, u32[]{:S(2)}, u32[]{:S(2)}) async-start(bf16[128,4,128]{2,1,0:T(4,128)(2,1)} %bitcast.13), calls=%async_computation.1 | async-start | bytes 262144 | tf_op jit(solution)/shard_map/all_to_all | solution.py:83
  44.0 1.3 reduce.3
  46.4 51.7 %while.22 = (s32[]{:T(128)}, f32[256,128]{1,0:T(8,128)S(1)}, s32[27,256]{1,0:T(8,128)S(1)}, bf16[385,128]{1,0:T(8,128)(2,1)S(1)}, bf16[27,128,128]{2,1,0:T(8,128)(2,1)}, /*index=5*/s32[]{:T(128)}, s32[]{:T(128)}) while((s32[]{:T(128)}, f32[256,128]{1,0:T(8,128)S(1)}, s32[27,256]{1,0:T(8,128)S(1)}, bf16[385,128]{1,0:T(8,128)(2,1)S(1)}, ...), condition=%wide.region_1.3_spmd.clone, body=%wide.region_0.2_spmd.clone.sunk | while | flops 8490243 | bytes 503399 | solution.py:57
  47.3 1.0 convolution_add_fusion.2
  49.2 1.0 convolution_add_fusion.2
  51.1 1.0 convolution_add_fusion.2
  53.0 1.0 convolution_add_fusion.2
  55.0 1.0 convolution_add_fusion.2
  56.9 1.0 convolution_add_fusion.2
  58.8 1.0 convolution_add_fusion.2
  60.7 1.0 convolution_add_fusion.2
  62.6 1.0 convolution_add_fusion.2
  64.5 1.0 convolution_add_fusion.2
  66.4 1.0 convolution_add_fusion.2
  68.4 1.0 convolution_add_fusion.2
  70.3 1.0 convolution_add_fusion.2
  72.2 1.0 convolution_add_fusion.2
  74.1 1.0 convolution_add_fusion.2
  76.0 1.0 convolution_add_fusion.2
  77.9 1.0 convolution_add_fusion.2
  79.8 1.0 convolution_add_fusion.2
  81.8 1.0 convolution_add_fusion.2
  83.7 1.0 convolution_add_fusion.2
  85.6 1.0 convolution_add_fusion.2
  87.5 1.0 convolution_add_fusion.2
  89.4 1.0 convolution_add_fusion.2
  91.3 1.0 convolution_add_fusion.2
  93.2 1.0 convolution_add_fusion.2
  95.2 1.0 convolution_add_fusion.2
  97.1 1.0 convolution_add_fusion.2
  98.1 1.9 scatter_custom_fusion
  100.0 13.7 %all-to-all-start = ((bf16[128,4,128]{2,1,0:T(4,128)(2,1)}), bf16[128,4,128]{2,1,0:T(4,128)(2,1)S(1)}, u32[]{:S(2)}, u32[]{:S(2)}) async-start(bf16[128,4,128]{2,1,0:T(4,128)(2,1)} %bitcast.6), calls=%async_computation | async-start | bytes 262144 | tf_op jit(solution)/shard_map/all_to_all | solution.py:66
  114.7 49.0 %while.21 = (s32[]{:T(128)}, f32[27,128,128]{2,1,0:T(8,128)}, s32[27,256]{1,0:T(8,128)S(1)}, bf16[385,128]{1,0:T(8,128)(2,1)S(1)}, bf16[256,128]{1,0:T(8,128)(2,1)S(1)}, /*index=5*/s32[]{:T(128)}) while((s32[]{:T(128)}, f32[27,128,128]{2,1,0:T(8,128)}, s32[27,256]{1,0:T(8,128)S(1)}, bf16[385,128]{1,0:T(8,128)(2,1)S(1)}, ...), condition=%wide.region_5.7_spmd, body=%wide.region_4.6_spmd.sunk | while | flops 8424706 | bytes 339541 | solution.py:100
  115.7 0.9 fusion.39
  117.5 0.9 fusion.39
  119.3 0.9 fusion.39
  121.1 0.9 fusion.39
  122.9 0.9 fusion.39
  124.7 0.9 fusion.39
  130.2 0.9 fusion.39
  135.6 0.9 fusion.39
  137.4 0.9 fusion.39
  141.0 0.9 fusion.39
  142.9 0.9 fusion.39
  146.5 0.9 fusion.39
  148.3 0.9 fusion.39
  150.1 0.9 fusion.39
  153.7 0.9 fusion.39
  155.5 0.9 fusion.39
  157.4 0.9 fusion.39
  159.2 0.9 fusion.39
  161.0 0.9 fusion.39
  162.8 0.9 fusion.39
  163.7 1.3 gather_fusion.2
  165.2 1.3 fusion.13
  167.6 280.3 %all-reduce.3.cloned.1.call-done = (f32[27,128,128]{2,1,0:T(8,128)}, f32[1024,256]{1,0:T(8,128)}) async-done(((f32[27,128,128]{2,1,0:T(8,128)}, f32[1024,256]{1,0:T(8,128)}), (f32[27,128,128]{2,1,0:T(8,128)}, f32[1024,256]{1,0:T(8,128)})) %all-reduce.3.cloned.1.call-update) | async-done | bytes 2818064 | tf_op jit(solution)/shard_map/psum | solution.py:101
  447.9 3.0 copy.42
  450.8 1.0 copy.43
  (311 shorter events, 59.9 us)
Async XLA Ops:
  7.2 16.3 %copy-start = (bf16[1024,256]{1,0:T(8,128)(2,1)S(1)}, bf16[1024,256]{1,0:T(8,128)(2,1)}, u32[]{:S(2)}) copy-start(bf16[1024,256]{1,0:T(8,128)(2,1)} %param.20) | copy-start | bytes 1572868
  12.7 33.5 %collective-permute-start = (bf16[64,128]{1,0:T(8,128)(2,1)S(1)}, bf16[64,128]{1,0:T(8,128)(2,1)S(1)}, u32[]{:S(2)}, u32[]{:S(2)}) collective-permute-start(bf16[64,128]{1,0:T(8,128)(2,1)S(1)} %get-tuple-element.102), channel_id=1, source_target_pairs={{0,4},{4,8},{8,12},{12,16},{16,20},{20,24},{24,28},{28,32},{32,36}... | collective-permute-start | bytes 49160 | tf_op jit(solution)/shard_map/ppermute | solution.py:15
  17.3 28.9 %collective-permute-start.1 = (bf16[64,128]{1,0:T(8,128)(2,1)S(1)}, bf16[64,128]{1,0:T(8,128)(2,1)S(1)}, u32[]{:S(2)}, u32[]{:S(2)}) collective-permute-start(bf16[64,128]{1,0:T(8,128)(2,1)S(1)} %get-tuple-element.103), channel_id=1, source_target_pairs={{4,0},{8,4},{12,8},{16,12},{20,16},{24,20},{28,24},{32,28},{36,32}... | collective-permute-start | bytes 49160 | tf_op jit(solution)/shard_map/ppermute | solution.py:18
  26.9 73.0 %all-to-all-start.1 = ((bf16[128,4,128]{2,1,0:T(4,128)(2,1)}), bf16[128,4,128]{2,1,0:T(4,128)(2,1)S(1)}, u32[]{:S(2)}, u32[]{:S(2)}) async-start(bf16[128,4,128]{2,1,0:T(4,128)(2,1)} %bitcast.13), calls=%async_computation.1 | async-start | bytes 262144 | tf_op jit(solution)/shard_map/all_to_all | solution.py:83
  100.0 63.8 %all-to-all-start = ((bf16[128,4,128]{2,1,0:T(4,128)(2,1)}), bf16[128,4,128]{2,1,0:T(4,128)(2,1)S(1)}, u32[]{:S(2)}, u32[]{:S(2)}) async-start(bf16[128,4,128]{2,1,0:T(4,128)(2,1)} %bitcast.6), calls=%async_computation | async-start | bytes 262144 | tf_op jit(solution)/shard_map/all_to_all | solution.py:66
  113.7 334.2 %all-reduce.3.cloned.1.call-start = ((), (), s32[]{:S(2)}) async-start(), calls=%async_computation.2 | async-start | bytes 5636096 | tf_op jit(solution)/shard_map/psum | solution.py:101
  114.7 50.5 %copy-start.2 = (bf16[1,64,256]{2,1,0:T(8,128)(2,1)S(1)}, bf16[1,64,256]{2,1,0:T(8,128)(2,1)}, u32[]{:S(2)}) copy-start(bf16[1,64,256]{2,1,0:T(8,128)(2,1)} %param.21) | copy-start | bytes 98308
  447.8 3.0 copy-start.1
Sparse Core Ops, SparseCore 0:
  166.7 281.1 all-reduce.2
where the time goes:
time: 461 us; the launch traced here: 459 us
  waiting for transfers between devices  280 us (61%)
  local copies, waits for them, and re-layouts  57.3 us (12%)
  matrix products  54.3 us (12%)
  starting transfers between devices  39 us (8%)
  between operations  17.5 us (4%)
  other arithmetic  8.4 us (2%)
    psum x1, waiting for transfers between devices, body(): grad_conv, grad_down = lax.psum((grad_conv, grad_down), ('blk', 'dp'))  280 us
    dot_general x27, matrix products, forward_step(): jnp.dot(picked, weight, preferred_element_type=jnp.float32)  26.4 us
    dot_general x27, matrix products, backward_step(): lax.dot_general(picked, grad_pre, (((0,), (0,)), ((), ())), preferred_ele...  24.8 us
    gather x27, local copies, waits for them, and re-layouts, backward_step(): picked = jnp.take(table, index_row, axis=0)  23.1 us
    gather x27, local copies, waits for them, and re-layouts, forward_step(): picked = jnp.take(table, index_row, axis=0)  23.1 us
    all_to_all x1, starting transfers between devices, body(): lax.all_to_all(returned, 'blk', split_axis=0, concat_axis=0, tiled=True)  15.1 us
    all_to_all x1, starting transfers between devices, body(): lax.all_to_all(outgoing, 'blk', split_axis=0, concat_axis=0, tiled=True)  13.7 us
  transfers between devices with their start and end apart: 5, of which 1 were waited for; matrix products, arithmetic and copies ran while one was open for 24% of the time, Pallas kernels for 0%

commit v1 on v0

v1 whole, which is shorter than its diff:
```python
import functools
import math

import jax
import jax.numpy as jnp
from jax import lax
from jax.experimental import pallas as pl
from jax.experimental.pallas import tpu as pltpu
from jax.sharding import PartitionSpec as P

OCT = 8
HALO = 64
F32 = jnp.float32
BF16 = jnp.bfloat16
MESH = pl.DeviceIdType.MESH


def iota(shape, dim):
    return lax.broadcasted_iota(jnp.int32, shape, dim)


def dot(a, b, ca, cb):
    return lax.dot_general(a, b, (((ca,), (cb,)), ((), ())), preferred_element_type=F32)


def up16(rows):
    return -(-rows // 16) * 16


class Place:
    def __init__(self, n, nx):
        blk = lax.axis_index("blk")
        self.n, self.nx = n, nx
        self.blk, self.x = blk, lax.axis_index("dp")
        self.c = lax.rem(blk, 2)
        chip = lax.div(blk, 2)
        z, y = lax.div(chip, n), lax.rem(chip, n)
        self.a = (1 - self.c) * y + self.c * z
        self.b = (1 - self.c) * z + self.c * y

    def of(self, a, b):
        c, n = self.c, self.n
        return ((1 - c) * (b * n + a) + c * (a * n + b)) * 2 + c

    def along_a(self, p):
        return (self.of(lax.rem(self.a + p, self.n), self.b), self.x)

    def along_b(self, p):
        return (self.of(self.a, lax.rem(self.b + p, self.n)), self.x)

    def along_x(self, p):
        return (self.blk, lax.rem(self.x + p, self.nx))

    def other_core(self):
        return (self.blk + 1 - 2 * self.c, self.x)

    def next_block(self, p, count):
        return (lax.rem(self.blk + p, count), self.x)


class Sender:
    def __init__(self, send_sem, recv_sem):
        self.send_sem, self.recv_sem, self.used, self.all = send_sem, recv_sem, 0, []

    def start(self, src, dst, device):
        copy = pltpu.make_async_remote_copy(
            src_ref=src,
            dst_ref=dst,
            send_sem=self.send_sem.at[self.used],
            recv_sem=self.recv_sem.at[self.used],
            device_id=device,
            device_id_type=MESH,
        )
        self.used += 1
        copy.start()
        self.all.append(copy)
        return copy

    def finish(self):
        for copy in self.all:
            copy.wait_send()


def arrived(copies):
    for copy in copies:
        copy.wait_recv()


class Exchange:
    def __init__(self, place, sender, bufs):
        self.place, self.sender = place, sender
        self.send1, self.recv1, self.send2, self.recv2, self.got = bufs

    def start(self, rows):
        pc, n = self.place, self.place.n
        self.send1[...] = rows.reshape(self.send1.shape)
        self.copies = [
            self.sender.start(
                self.send1.at[lax.rem(pc.a + p, n)], self.recv1.at[pc.a], pc.along_a(p)
            )
            for p in range(1, n)
        ]
        self.recv1[pc.a] = self.send1[pc.a]

    def second(self, swap):
        pc, n = self.place, self.place.n
        arrived(self.copies)
        flat = self.recv1[...].reshape(swap.shape[1], -1)
        moved = jnp.dot(swap[...], flat, preferred_element_type=F32).astype(BF16)
        self.send2[...] = moved.reshape(self.send2.shape)
        self.copies = [
            self.sender.start(
                self.send2.at[lax.rem(pc.b + p, n)], self.recv2.at[pc.b], pc.along_b(p)
            )
            for p in range(1, n)
        ]
        self.recv2[pc.b] = self.send2[pc.b]

    def third(self):
        pc = self.place
        arrived(self.copies)
        self.copies = [
            self.sender.start(self.recv2.at[:, 1 - pc.c], self.got.at[pc.c], pc.other_core())
        ]
        self.got[pc.c] = self.recv2[:, pc.c]

    def result(self):
        arrived(self.copies)
        flat = self.got[...]
        return flat.reshape(-1, flat.shape[-1])


class Sum:
    def __init__(self, place, sender, rows, bufs, out):
        self.place, self.sender, self.rows, self.out = place, sender, rows, out
        n = place.n
        self.part = up16(-(-rows // n))
        self.wide = up16(rows)
        self.s0, self.r0, self.own, self.s1, self.r1 = bufs[:5]
        self.s2, self.r2, self.s3, self.g2, self.g1 = bufs[5:]

    @staticmethod
    def scratch(rows, n, nx):
        part, wide = up16(-(-rows // n)), up16(rows)
        return [
            pltpu.VMEM((n * rows, 128), BF16),
            pltpu.VMEM((n * rows, 128), BF16),
            pltpu.VMEM((n * rows, 128), F32),
            pltpu.VMEM((n, wide, 128), BF16),
            pltpu.VMEM((n, wide, 128), BF16),
            pltpu.VMEM((n, part, 128), F32),
            pltpu.VMEM((n, part, 128), F32),
            pltpu.VMEM((nx, part, 128), F32),
            pltpu.VMEM((n * part, 128), BF16),
            pltpu.VMEM((n, wide, 128), BF16),
        ]

    def start(self, theirs, mine):
        self.s0[...] = theirs().astype(BF16)
        self.copies = [self.sender.start(self.s0, self.r0, self.place.other_core())]
        self.own[...] = mine()

    def along_a(self):
        pc, n, rows = self.place, self.place.n, self.rows
        arrived(self.copies)
        for q in range(n):
            chunk = pl.ds(q * rows, rows)
            total = self.own[chunk] + self.r0[chunk].astype(F32)
            self.own[chunk] = total
            self.s1[q, pl.ds(0, rows)] = total.astype(BF16)
            if self.wide > rows:
                self.s1[q, pl.ds(rows, self.wide - rows)] = jnp.zeros(
                    (self.wide - rows, 128), BF16
                )
        self.copies = [
            self.sender.start(
                self.s1.at[lax.rem(pc.a + p, n)], self.r1.at[p], pc.along_a(p)
            )
            for p in range(1, n)
        ]

    def along_b(self):
        pc, n, rows = self.place, self.place.n, self.rows
        arrived(self.copies)
        total = self.own[pl.ds(pl.multiple_of(pc.a * rows, 8), rows)]
        for p in range(1, n):
            total += self.r1[p][:rows].astype(F32)
        spare = n * self.part - rows
        if spare:
            total = jnp.concatenate([total, jnp.zeros((spare, 128), F32)], 0)
        self.s2[...] = total.reshape(self.s2.shape)
        self.copies = [
            self.sender.start(
                self.s2.at[lax.rem(pc.b + p, n)], self.r2.at[p], pc.along_b(p)
            )
            for p in range(1, n)
        ]

    def along_x(self):
        pc, n = self.place, self.place.n
        arrived(self.copies)
        total = self.s2[pc.b]
        for p in range(1, n):
            total += self.r2[p]
        self.s3[pc.x] = total
        self.copies = [
            self.sender.start(self.s3.at[pc.x], self.s3.at[pc.x], pc.along_x(p))
            for p in range(1, pc.nx)
        ]

    def back_b(self):
        pc, n = self.place, self.place.n
        arrived(self.copies)
        total = self.s3[0]
        for x in range(1, pc.nx):
            total += self.s3[x]
        mine = pl.ds(pl.multiple_of(pc.b * self.part, 16), self.part)
        self.g2[mine] = total.astype(BF16)
        self.copies = [
            self.sender.start(self.g2.at[mine], self.g2.at[mine], pc.along_b(p))
            for p in range(1, n)
        ]

    def back_a(self):
        pc, n = self.place, self.place.n
        arrived(self.copies)
        self.g1[pc.a] = self.g2[pl.ds(0, self.wide)]
        self.copies = [
            self.sender.start(self.g1.at[pc.a], self.g1.at[pc.a], pc.along_a(p))
            for p in range(1, n)
        ]

    def back_core(self, sem):
        pc = self.place
        arrived(self.copies)
        self.copies = [self.sender.start(self.g1, self.out.at[pc.c], pc.other_core())]
        self.kept = pltpu.make_async_copy(self.g1, self.out.at[pc.c], sem)
        self.kept.start()

    def result(self):
        arrived(self.copies)
        self.kept.wait()


def kernel(n, nx, cap, *refs):
    (
        features,
        kernel_map,
        block_counts,
        send_position,
        cell_source,
        conv_weight,
        down_weight,
        cotangent,
        coarse,
        out_conv,
        out_down,
        table,
        index,
        weight_t,
        picked,
        by_child,
        send_hot,
        swap,
        down_grad,
        *rest,
    ) = refs
    *rest, send_sem, recv_sem, local_sem = rest
    count = 2 * n * n
    offsets = conv_weight.shape[0]
    rows, width = features.shape[1], features.shape[2]
    cells = n * n * 2 * cap
    taps = offsets * width
    half = taps // 2
    pc = Place(n, nx)
    sender = Sender(send_sem, recv_sem)

    barrier = pltpu.get_barrier_semaphore()
    partners = [pc.along_a(p) for p in range(1, n)] + [pc.along_b(p) for p in range(1, n)]
    partners += [pc.along_x(p) for p in range(1, nx)]
    partners += [pc.other_core(), pc.next_block(1, count), pc.next_block(count - 1, count)]
    for device in partners:
        pl.semaphore_signal(barrier, inc=1, device_id=device, device_id_type=MESH)

    counted = block_counts[0, pc.blk]
    front = lax.div(counted, 2)
    back = rows - (counted - front)
    down = iota((rows, width), 0)
    live = (down < front) | (down >= back)
    across = iota((1, rows), 1)
    live_t = (across < front) | (across >= back)
    masked = jnp.where(live, features[0].astype(F32), 0.0)
    table[pl.ds(HALO, rows)] = masked.astype(BF16)
    pl.semaphore_wait(barrier, len(partners))

    halo = [
        sender.start(
            table.at[pl.ds(rows, HALO)], table.at[pl.ds(0, HALO)], pc.next_block(1, count)
        ),
        sender.start(
            table.at[pl.ds(HALO, HALO)],
            table.at[pl.ds(HALO + rows, HALO)],
            pc.next_block(count - 1, count),
        ),
    ]

    forward = Exchange(pc, sender, rest[0:5])
    backward = Exchange(pc, sender, rest[5:10])
    sum_conv = Sum(pc, sender, half // n, rest[10:20], out_conv)
    sum_down = Sum(pc, sender, OCT * width // n, rest[20:30], out_down)

    r = iota((cells, 1), 0)
    slot, r1 = lax.rem(r, cap), lax.div(r, cap)
    to_b, r2 = lax.rem(r1, n), lax.div(r1, n)
    to_c, to_a = lax.rem(r2, 2), lax.div(r2, 2)
    chip = jnp.where(pc.c == 0, to_b * n + to_a, to_a * n + to_b)
    goes_to = (chip * 2 + to_c) * cap + slot
    from_a, from_b, from_c = to_b, lax.rem(r2, n), lax.div(r2, n)
    chip = jnp.where(from_c == 0, from_b * n + from_a, from_a * n + from_b)
    comes_from = (chip * 2 + from_c) * cap + slot

    def hot(at, values):
        return jnp.where(at == values, 1.0, 0.0).astype(BF16)

    for j in range(OCT):
        part = dot(cotangent[0], down_weight[pl.ds(j * width, width)], 1, 1)
        by_child[pl.ds(j, rows // 4, stride=OCT)] = part.astype(BF16).astype(F32)
    children = cell_source[...]
    backward.start(
        jnp.dot(hot(goes_to, children), by_child[...].astype(BF16), preferred_element_type=F32)
        .astype(BF16)
    )

    swapped = ((to_b * 2 + to_c) * n + to_a) * cap + slot
    swap[...] = hot(swapped, iota((1, cells), 1))
    position = send_position[...]
    send_hot[...] = hot(goes_to, position)
    for k in range(offsets):
        weight_t[:, pl.ds(k * width, width)] = conv_weight[k].astype(F32).T.astype(BF16)
    entry = kernel_map[0]
    lane = lax.rem(iota(entry.shape, 1), 128)
    index[...] = jnp.where(entry >= 0, entry + lane, -1)

    arrived(halo)
    table_t = table[...].astype(F32).T.astype(BF16)
    window = iota((2 * HALO + 128, 128), 0)
    for k in range(offsets):
        for t in range(rows // 128):
            chosen = hot(window, index[pl.ds(k, 1), pl.ds(t * 128, 128)])
            got = jnp.dot(
                table_t[:, t * 128 : t * 128 + 128 + 2 * HALO], chosen, preferred_element_type=F32
            )
            picked[pl.ds(k * width, width), pl.ds(t * 128, 128)] = got.astype(BF16)

    backward.second(swap)
    pre = jnp.dot(weight_t[...], picked[...], preferred_element_type=F32)
    sig = 1.0 / (1.0 + jnp.exp(-pre))
    hidden = jnp.where(live_t, pre * sig, 0.0).astype(BF16)
    forward.start(dot(send_hot[...], hidden, 1, 1).astype(BF16))

    backward.third()
    from_owner = hot(comes_from, position)
    slope = jnp.where(live_t, sig * (1.0 + pre * (1.0 - sig)), 0.0)
    grad_hidden = dot(backward.result(), from_owner, 0, 0)
    grad_pre = (grad_hidden * slope).astype(BF16)

    def conv_half(h):
        chosen = picked[pl.ds(pl.multiple_of(h * half, 16), half)]
        return dot(chosen, grad_pre, 1, 1)

    sum_conv.start(lambda: conv_half(1 - pc.c), lambda: conv_half(pc.c))
    forward.second(swap)
    sum_conv.along_a()
    forward.third()

    to_child = hot(comes_from, children)
    by_child[...] = dot(to_child, forward.result(), 0, 0)
    total = jnp.zeros(coarse.shape[1:], F32)
    for j in range(OCT):
        child = by_child[pl.ds(j, rows // 4, stride=OCT)].astype(BF16)
        grad = dot(child, cotangent[0], 0, 0)
        for h in range(2):
            down_grad[h, pl.ds(j * width, width)] = grad[:, h * 128 : (h + 1) * 128]
        total += jnp.dot(
            child, down_weight[pl.ds(j * width, width)], preferred_element_type=F32
        )
    sum_down.start(lambda: down_grad[1 - pc.c], lambda: down_grad[pc.c])
    coarse[0] = total.astype(BF16)

    sum_conv.along_b()
    sum_down.along_a()
    sum_conv.along_x()
    sum_down.along_b()
    sum_conv.back_b()
    sum_down.along_x()
    sum_conv.back_a()
    sum_down.back_b()
    sum_conv.back_core(local_sem.at[0])
    sum_down.back_a()
    sum_down.back_core(local_sem.at[1])
    sum_conv.result()
    sum_down.result()
    sender.finish()


def body(n, nx, *args):
    features, kernel_map, _, _, cell_source, conv_weight, down_weight, cotangent = args
    rows, width = features.shape[1:]
    offsets = conv_weight.shape[0]
    cells = cell_source.shape[1]
    cap = cells // (2 * n * n)
    half = offsets * width // 2
    exchange = [
        pltpu.VMEM((n, cells // n, width), BF16),
        pltpu.VMEM((n, cells // n, width), BF16),
        pltpu.VMEM((n, 2, cells // n // 2, width), BF16),
        pltpu.VMEM((n, 2, cells // n // 2, width), BF16),
        pltpu.VMEM((2, n, cells // n // 2, width), BF16),
    ]
    copies = 2 + 2 * (2 * (n - 1) + 1) + 2 * (4 * (n - 1) + nx - 1 + 2)
    vmem = pl.BlockSpec(memory_space=pltpu.VMEM)
    conv_rows, down_rows = half // n, OCT * width // n
    coarse, conv, down = pl.pallas_call(
        functools.partial(kernel, n, nx, cap),
        out_shape=[
            jax.ShapeDtypeStruct(cotangent.shape, BF16),
            jax.ShapeDtypeStruct((2, n, up16(conv_rows), 128), BF16),
            jax.ShapeDtypeStruct((2, n, up16(down_rows), 128), BF16),
        ],
        in_specs=[vmem, vmem, pl.BlockSpec(memory_space=pltpu.SMEM)] + [vmem] * 5,
        out_specs=[vmem, pl.BlockSpec(memory_space=pl.ANY), pl.BlockSpec(memory_space=pl.ANY)],
        scratch_shapes=[
            pltpu.VMEM((rows + 2 * HALO, width), BF16),
            pltpu.VMEM((offsets, rows), jnp.int32),
            pltpu.VMEM((width, offsets * width), BF16),
            pltpu.VMEM((offsets * width, rows), BF16),
            pltpu.VMEM((cells, width), F32),
            pltpu.VMEM((cells, rows), BF16),
            pltpu.VMEM((cells, cells), BF16),
            pltpu.VMEM((2, OCT * width, 128), F32),
            *exchange,
            *exchange,
            *Sum.scratch(conv_rows, n, nx),
            *Sum.scratch(down_rows, n, nx),
            pltpu.SemaphoreType.DMA((copies,)),
            pltpu.SemaphoreType.DMA((copies,)),
            pltpu.SemaphoreType.DMA((2,)),
        ],
        compiler_params=pltpu.CompilerParams(
            collective_id=0, has_side_effects=True, vmem_limit_bytes=48 << 20
        ),
    )(*args)
    grad_conv = conv[:, :, :conv_rows].astype(F32).reshape(offsets, width, width)
    grad_down = jnp.concatenate([down[0], down[1]], -1).astype(F32).reshape(OCT * width, 256)
    return (coarse, grad_conv, grad_down)


def solution(mesh):
    n, nx = math.isqrt(mesh.shape["blk"] // 2), mesh.shape["dp"]
    in_specs = (
        P("dp", "blk", None),
        P("dp", None, "blk"),
        P("dp", None),
        P("dp", "blk"),
        P("dp", "blk"),
        P(),
        P(),
        P("dp", "blk", None),
    )
    out_specs = (P("dp", "blk", None), P(), P())
    return jax.shard_map(
        functools.partial(body, n, nx),
        mesh=mesh,
        in_specs=in_specs,
        out_specs=out_specs,
        check_vma=False,
    )
```

time: 461 us -> 88.8 us (0.19)
  waiting for transfers between devices: 280 us -> 0 us
  Pallas kernels: 0 us -> 77.9 us
  matrix products: 54.3 us -> 0 us
  local copies, waits for them, and re-layouts: 57.3 us -> 7.28 us
  starting transfers between devices: 39 us -> 0 us
  between operations: 17.5 us -> 0.66 us
  other arithmetic: 8.4 us -> 2.45 us
    psum x1 -> x0, waiting for transfers between devices: 280 us -> none  [body(): grad_conv, grad_down = lax.psum((grad_conv, grad_down), ('blk', 'dp'))]
    pallas_call x0 -> x1, Pallas kernels: none -> 77.9 us  [body(): pl.pallas_call(functools.partial(kernel, n, nx, cap), out_shape=[jax.Shap...]
    dot_general x57 -> x0, matrix products: 54.3 us -> none  [the longest x27 26.4 us: forward_step(): jnp.dot(picked, weight, preferred_element_type=jnp.float32)]
    gather x57 -> x0, local copies, waits for them, and re-layouts: 48.4 us -> none  [the longest x27 23.1 us: backward_step(): picked = jnp.take(table, index_row, axis=0)]
    all_to_all x2 -> x0, starting transfers between devices: 28.8 us -> none  [the longest x1 15.1 us: body(): lax.all_to_all(returned, 'blk', split_axis=0, concat_axis=0, tiled=True)]
    ppermute x2 -> x0, starting transfers between devices: 10.1 us -> none  [the longest x1 5.48 us: with_halo(): lax.ppermute(lax.slice_in_dim(block, 0, width, axis=dim), axis, backward)]
  transfers between devices with their start and end apart: 5 -> 0, of which waited for: 1 -> 0; matrix products, arithmetic and copies ran while one was open for 24% -> 0% of each run, Pallas kernels for 0% -> 0%
where the time goes in v1:
time: 88.8 us; the launch traced here: 88.3 us
  Pallas kernels  77.9 us (88%)
  local copies, waits for them, and re-layouts  7.28 us (8%)
  other arithmetic  2.45 us (3%)
    pallas_call x1, Pallas kernels, body(): pl.pallas_call(functools.partial(kernel, n, nx, cap), out_shape=[jax.Shap...  77.9 us
    unnamed x16, local copies, waits for them, and re-layouts  7.18 us

profile of v1, /device:TPU:1, one launch (start us, length us, event | category | flops | bytes accessed | tf_op | source)
XLA Modules:
  0.0 88.3 jit_solution(12743661504483203470)
XLA Ops:
  0.6 0.7 copy.11.refs_1_
  1.4 0.0 copy-start
  1.4 1.2 %copy-done = bf16[27,128,128]{2,1,0:T(8,128)(2,1)S(1)} copy-done((bf16[27,128,128]{2,1,0:T(8,128)(2,1)S(1)}, bf16[27,128,128]{2,1,0:T(8,128)(2,1)}, u32[]{:S(2)}) %copy-start) | copy-done | bytes 884760
  2.5 0.0 copy-start.1
  2.5 1.0 %copy-done.1 = bf16[1024,256]{1,0:T(8,128)(2,1)S(1)} copy-done((bf16[1024,256]{1,0:T(8,128)(2,1)S(1)}, bf16[1024,256]{1,0:T(8,128)(2,1)}, u32[]{:S(2)}) %copy-start.1) | copy-done | bytes 524312
  3.6 0.0 copy-start.2
  3.6 0.8 copy-done.2
  4.4 0.0 copy-start.3
  4.4 0.8 copy-done.3
  5.2 0.0 copy-start.4
  5.2 0.7 copy-done.4
  5.9 0.0 copy-start.5
  5.9 0.7 copy-done.5
  6.5 0.0 copy-start.6
  6.6 0.7 copy-done.6
  7.2 77.9 %shard_map.103 = (bf16[1,64,256]{2,1,0:T(8,128)(2,1)S(1)}, bf16[2,8,224,128]{3,2,1,0:T(8,128)(2,1)S(1)}, bf16[2,8,128,128]{3,2,1,0:T(8,128)(2,1)S(1)}) custom-call(bf16[1,256,128]{2,1,0:T(8,128)(2,1)S(1)} %copy-done.2, s32[1,27,256]{2,1,0:T(8,128)S(1)} %copy.11.refs_1_, s32[1,128]{1,0:T(1,128)S(1)} %copy-done.6, s32[1,256]{1,0:T(1,128)S(1)} %copy-done.5, ...), custom_call_target="tpu_custom_call" | custom-call | tf_op jit(solution)/shard_map/pallas_call | solution.py:423
  85.2 0.1 slice.9
  85.2 1.4 %convert.1 = f32[27,128,128]{2,1,0:T(8,128)} convert(bf16[27,128,128]{2,1,0:T(8,128)(2,1)S(1)} %bitcast.4) | non-fusion elementwise | flops 442368 | bytes 2654208 | tf_op jit(solution)/shard_map/reshape | solution.py:453
  86.7 1.0 %maximum_convert_fusion = f32[1024,256]{1,0:T(8,128)} fusion(bf16[1024,128]{1,0:T(8,128)(2,1)S(1)} %bitcast.6, bf16[1024,128]{1,0:T(8,128)(2,1)S(1)} %bitcast.5), kind=kLoop, calls=%fused_computation | loop fusion | flops 1048576 | bytes 1572864 | tf_op jit(solution)/shard_map/convert_element_type | solution.py:454
  87.7 0.6 copy.13
  (1 shorter events, 0.0 us)
Async XLA Ops:
  1.4 1.2 %copy-start = (bf16[27,128,128]{2,1,0:T(8,128)(2,1)S(1)}, bf16[27,128,128]{2,1,0:T(8,128)(2,1)}, u32[]{:S(2)}) copy-start(bf16[27,128,128]{2,1,0:T(8,128)(2,1)} %refs_5_.1) | copy-start | bytes 2654212
  2.5 1.0 %copy-start.1 = (bf16[1024,256]{1,0:T(8,128)(2,1)S(1)}, bf16[1024,256]{1,0:T(8,128)(2,1)}, u32[]{:S(2)}) copy-start(bf16[1024,256]{1,0:T(8,128)(2,1)} %refs_6_.1) | copy-start | bytes 1572868
  3.6 0.8 copy-start.2
  4.4 0.8 copy-start.3
  5.2 0.7 copy-start.4
  5.9 0.7 copy-start.5
  6.5 0.7 copy-start.6

commit v2 on v1

v2 whole, which is shorter than its diff:
```python
import functools
import math

import jax
import jax.numpy as jnp
from jax import lax
from jax.experimental import pallas as pl
from jax.experimental.pallas import tpu as pltpu
from jax.sharding import PartitionSpec as P

OCT = 8
HALO = 64
F32 = jnp.float32
BF16 = jnp.bfloat16
MESH = pl.DeviceIdType.MESH


def iota(shape, dim):
    return lax.broadcasted_iota(jnp.int32, shape, dim)


def dot(a, b, ca, cb):
    return lax.dot_general(a, b, (((ca,), (cb,)), ((), ())), preferred_element_type=F32)


def up16(rows):
    return -(-rows // 16) * 16


class Place:
    def __init__(self, n, nx):
        blk = lax.axis_index("blk")
        self.n, self.nx = n, nx
        self.blk, self.x = blk, lax.axis_index("dp")
        self.c = lax.rem(blk, 2)
        chip = lax.div(blk, 2)
        z, y = lax.div(chip, n), lax.rem(chip, n)
        self.a = (1 - self.c) * y + self.c * z
        self.b = (1 - self.c) * z + self.c * y

    def of(self, a, b):
        c, n = self.c, self.n
        return ((1 - c) * (b * n + a) + c * (a * n + b)) * 2 + c

    def axis(self, name):
        if name == "x":
            return self.nx, self.x, self.along_x
        return (self.n, self.a, self.along_a) if name == "a" else (self.n, self.b, self.along_b)

    def along_a(self, p):
        return (self.of(lax.rem(self.a + p, self.n), self.b), self.x)

    def along_b(self, p):
        return (self.of(self.a, lax.rem(self.b + p, self.n)), self.x)

    def along_x(self, p):
        return (self.blk, lax.rem(self.x + p, self.nx))

    def other_core(self):
        return (self.blk + 1 - 2 * self.c, self.x)

    def next_block(self, p, count):
        return (lax.rem(self.blk + p, count), self.x)


class Sender:
    def __init__(self, send_sem, recv_sem):
        self.send_sem, self.recv_sem, self.used, self.all = send_sem, recv_sem, 0, []

    def start(self, src, dst, device):
        copy = pltpu.make_async_remote_copy(
            src_ref=src,
            dst_ref=dst,
            send_sem=self.send_sem.at[self.used],
            recv_sem=self.recv_sem.at[self.used],
            device_id=device,
            device_id_type=MESH,
        )
        self.used += 1
        copy.start()
        self.all.append(copy)
        return copy

    def finish(self):
        for copy in self.all:
            copy.wait_send()


def arrived(copies):
    for copy in copies:
        copy.wait_recv()


class Exchange:
    def __init__(self, place, sender, bufs):
        self.place, self.sender = place, sender
        self.send1, self.recv1, self.send2, self.recv2, self.got = bufs

    def start(self, rows):
        pc, n = self.place, self.place.n
        self.send1[...] = rows.reshape(self.send1.shape)
        self.copies = [
            self.sender.start(
                self.send1.at[lax.rem(pc.a + p, n)], self.recv1.at[pc.a], pc.along_a(p)
            )
            for p in range(1, n)
        ]
        self.recv1[pc.a] = self.send1[pc.a]

    def second(self, swap):
        pc, n = self.place, self.place.n
        arrived(self.copies)
        flat = self.recv1[...].reshape(swap.shape[1], -1)
        moved = jnp.dot(swap[...], flat, preferred_element_type=F32).astype(BF16)
        self.send2[...] = moved.reshape(self.send2.shape)
        self.copies = [
            self.sender.start(
                self.send2.at[lax.rem(pc.b + p, n)], self.recv2.at[pc.b], pc.along_b(p)
            )
            for p in range(1, n)
        ]
        self.recv2[pc.b] = self.send2[pc.b]

    def third(self):
        pc = self.place
        arrived(self.copies)
        self.copies = [
            self.sender.start(self.recv2.at[:, 1 - pc.c], self.got.at[pc.c], pc.other_core())
        ]
        self.got[pc.c] = self.recv2[:, pc.c]

    def result(self):
        arrived(self.copies)
        flat = self.got[...]
        return flat.reshape(-1, flat.shape[-1])


class Sum:
    def __init__(self, place, sender, rows, order, bufs, out):
        self.place, self.sender, self.out = place, sender, out
        self.axes = [place.axis(name) for name in order]
        self.rows, self.part, self.wide = self.sizes(rows, *[axis[0] for axis in self.axes[:2]])
        self.s0, self.r0, self.own, self.s1, self.r1 = bufs[:5]
        self.s2, self.r2, self.s3, self.g2, self.g1 = bufs[5:]

    @staticmethod
    def sizes(rows, n1, n2):
        chunk = rows // n1
        return chunk, up16(-(-chunk // n2)), up16(chunk)

    @staticmethod
    def scratch(rows, n1, n2, n3):
        _, part, wide = Sum.sizes(rows, n1, n2)
        return [
            pltpu.VMEM((rows, 128), BF16),
            pltpu.VMEM((rows, 128), BF16),
            pltpu.VMEM((rows, 128), F32),
            pltpu.VMEM((n1, wide, 128), BF16),
            pltpu.VMEM((n1, wide, 128), BF16),
            pltpu.VMEM((n2, part, 128), F32),
            pltpu.VMEM((n2, part, 128), F32),
            pltpu.VMEM((n3, part, 128), F32),
            pltpu.VMEM((n2 * part, 128), BF16),
            pltpu.VMEM((n1, wide, 128), BF16),
        ]

    def start(self, theirs, mine):
        self.s0[...] = theirs().astype(BF16)
        self.copies = [self.sender.start(self.s0, self.r0, self.place.other_core())]
        self.own[...] = mine()

    def first(self):
        (n, me, along), rows = self.axes[0], self.rows
        arrived(self.copies)
        for q in range(n):
            chunk = pl.ds(q * rows, rows)
            total = self.own[chunk] + self.r0[chunk].astype(F32)
            self.own[chunk] = total
            self.s1[q, pl.ds(0, rows)] = total.astype(BF16)
            if self.wide > rows:
                self.s1[q, pl.ds(rows, self.wide - rows)] = jnp.zeros(
                    (self.wide - rows, 128), BF16
                )
        self.copies = [
            self.sender.start(self.s1.at[lax.rem(me + p, n)], self.r1.at[p], along(p))
            for p in range(1, n)
        ]

    def second(self):
        (n1, me1, _), (n, me, along), rows = self.axes[0], self.axes[1], self.rows
        arrived(self.copies)
        total = self.own[pl.ds(pl.multiple_of(me1 * rows, 8), rows)]
        for p in range(1, n1):
            total += self.r1[p][:rows].astype(F32)
        spare = n * self.part - rows
        if spare:
            total = jnp.concatenate([total, jnp.zeros((spare, 128), F32)], 0)
        self.s2[...] = total.reshape(self.s2.shape)
        self.copies = [
            self.sender.start(self.s2.at[lax.rem(me + p, n)], self.r2.at[p], along(p))
            for p in range(1, n)
        ]

    def third(self):
        (n2, me2, _), (n, me, along) = self.axes[1:]
        arrived(self.copies)
        total = self.s2[me2]
        for p in range(1, n2):
            total += self.r2[p]
        self.s3[me] = total
        self.copies = [
            self.sender.start(self.s3.at[me], self.s3.at[me], along(p)) for p in range(1, n)
        ]

    def back_second(self):
        n, me, along = self.axes[1]
        arrived(self.copies)
        total = self.s3[0]
        for x in range(1, self.axes[2][0]):
            total += self.s3[x]
        mine = pl.ds(pl.multiple_of(me * self.part, 16), self.part)
        self.g2[mine] = total.astype(BF16)
        self.copies = [
            self.sender.start(self.g2.at[mine], self.g2.at[mine], along(p)) for p in range(1, n)
        ]

    def back_first(self):
        n, me, along = self.axes[0]
        arrived(self.copies)
        self.g1[me] = self.g2[pl.ds(0, self.wide)]
        self.copies = [
            self.sender.start(self.g1.at[me], self.g1.at[me], along(p)) for p in range(1, n)
        ]

    def back_core(self, sem):
        pc = self.place
        arrived(self.copies)
        self.copies = [self.sender.start(self.g1, self.out.at[pc.c], pc.other_core())]
        self.kept = pltpu.make_async_copy(self.g1, self.out.at[pc.c], sem)
        self.kept.start()

    def result(self):
        arrived(self.copies)
        self.kept.wait()


def conv_split(rows):
    return rows * 13 // 27


ORDERS = (("a", "b", "x"), ("x", "a", "b"), ("x", "a", "b"))


def kernel(n, nx, cap, *refs):
    given, (out_coarse, *outs), refs = refs[:8], refs[8:12], refs[12:]
    (
        kernel_map,
        block_counts,
        send_position,
        cell_source,
        conv_weight,
        down_weight,
        cotangent,
        raw,
        weight_t,
        picked,
        by_child,
        send_hot,
        swap,
        down_grad,
        coarse,
        *rest,
    ) = refs
    *rest, send_sem, recv_sem, local_sem, load_sem = rest
    count = 2 * n * n
    features = given[0]
    offsets = conv_weight.shape[0]
    rows, width = features.shape[1], features.shape[2]
    cells = count * cap
    half = offsets * width // 2
    pc = Place(n, nx)
    sender = Sender(send_sem, recv_sem)

    barrier = pltpu.get_barrier_semaphore()
    partners = [pc.along_a(p) for p in range(1, n)] + [pc.along_b(p) for p in range(1, n)]
    partners += [pc.along_x(p) for p in range(1, nx)]
    partners += [pc.other_core(), pc.next_block(1, count), pc.next_block(count - 1, count)]
    for device in partners:
        pl.semaphore_signal(barrier, inc=1, device_id=device, device_id_type=MESH)

    targets = [raw.at[pl.ds(HALO, rows)], *refs[:7]]
    sources = [features.at[0], *given[1:]]
    loads = [
        pltpu.make_async_copy(src, dst, load_sem.at[i])
        for i, (src, dst) in enumerate(zip(sources, targets))
    ]
    for i in (7, 6, 4, 0, 2, 3, 1, 5):
        loads[i].start()
    pl.semaphore_wait(barrier, len(partners))

    halo = [
        sender.start(
            features.at[0, pl.ds(rows - HALO, HALO)],
            raw.at[pl.ds(0, HALO)],
            pc.next_block(1, count),
        ),
        sender.start(
            features.at[0, pl.ds(0, HALO)],
            raw.at[pl.ds(HALO + rows, HALO)],
            pc.next_block(count - 1, count),
        ),
    ]

    forward = Exchange(pc, sender, rest[0:5])
    backward = Exchange(pc, sender, rest[5:10])
    first_rows = conv_split(half)
    sums = [
        Sum(pc, sender, total, order, rest[10 + 10 * i : 20 + 10 * i], outs[i])
        for i, (total, order) in enumerate(
            zip((first_rows, half - first_rows, OCT * width), ORDERS)
        )
    ]
    sum_conv, sum_down = sums[:2], sums[2]

    r = iota((cells, 1), 0)
    slot, r1 = lax.rem(r, cap), lax.div(r, cap)
    to_b, r2 = lax.rem(r1, n), lax.div(r1, n)
    to_c, to_a = lax.rem(r2, 2), lax.div(r2, 2)
    chip = jnp.where(pc.c == 0, to_b * n + to_a, to_a * n + to_b)
    goes_to = (chip * 2 + to_c) * cap + slot
    from_a, from_b, from_c = to_b, lax.rem(r2, n), lax.div(r2, n)
    chip = jnp.where(from_c == 0, from_b * n + from_a, from_a * n + from_b)
    comes_from = (chip * 2 + from_c) * cap + slot

    def hot(at, values):
        return jnp.where(at == values, 1.0, 0.0).astype(BF16)

    for i in (7, 6, 4):
        loads[i].wait()
    for j in range(OCT):
        part = dot(cotangent[0], down_weight[pl.ds(j * width, width)], 1, 1)
        by_child[pl.ds(j, rows // 4, stride=OCT)] = part.astype(BF16).astype(F32)
    children = cell_source[...]
    backward.start(
        jnp.dot(hot(goes_to, children), by_child[...].astype(BF16), preferred_element_type=F32)
        .astype(BF16)
    )

    loads[0].wait()
    loads[2].wait()

    def live_of(block, inside):
        counted = block_counts[0, lax.rem(block, count)]
        front = lax.div(counted, 2)
        return (inside < front) | (inside >= rows - (counted - front))

    loads[5].wait()
    for k in range(offsets):
        weight_t[:, pl.ds(k * width, width)] = conv_weight[k].astype(F32).T.astype(BF16)
    loads[1].wait()
    lane = lax.rem(iota((1, rows), 1), 128)
    window = iota((2 * HALO + 128, 128), 0)
    live_t = live_of(pc.blk, iota((1, rows), 1))
    live = jnp.concatenate(
        [
            live_of(pc.blk + count - 1, iota((HALO, width), 0) + rows - HALO),
            live_of(pc.blk, iota((rows, width), 0)),
            live_of(pc.blk + 1, iota((HALO, width), 0)),
        ],
        0,
    )

    arrived(halo)
    table_t = jnp.where(live, raw[...].astype(F32), 0.0).T.astype(BF16)
    for k in range(offsets):
        entry = kernel_map[k]
        index = jnp.where(entry >= 0, entry + lane, -1)
        for t in range(rows // 128):
            chosen = hot(window, index[:, t * 128 : (t + 1) * 128])
            got = jnp.dot(
                table_t[:, t * 128 : t * 128 + 128 + 2 * HALO], chosen, preferred_element_type=F32
            )
            picked[pl.ds(k * width, width), pl.ds(t * 128, 128)] = got.astype(BF16)

    loads[3].wait()
    position = send_position[...]
    send_hot[...] = hot(goes_to, position)
    pre = jnp.dot(weight_t[...], picked[...], preferred_element_type=F32)
    sig = 1.0 / (1.0 + jnp.exp(-pre))
    hidden = jnp.where(live_t, pre * sig, 0.0).astype(BF16)
    forward.start(dot(send_hot[...], hidden, 1, 1).astype(BF16))

    swapped = ((to_b * 2 + to_c) * n + to_a) * cap + slot
    swap[...] = hot(swapped, iota((1, cells), 1))
    backward.second(swap)
    from_owner = hot(comes_from, position)
    slope = jnp.where(live_t, sig * (1.0 + pre * (1.0 - sig)), 0.0)
    forward.second(swap)
    backward.third()
    grad_hidden = dot(backward.result(), from_owner, 0, 0)
    grad_pre = (grad_hidden * slope).astype(BF16)

    def conv_rows(h, start, size):
        chosen = picked[pl.ds(pl.multiple_of(h * half + start, 16), size)]
        return dot(chosen, grad_pre, 1, 1)

    for job, start, size in (
        (sum_conv[0], 0, first_rows),
        (sum_conv[1], first_rows, half - first_rows),
    ):
        job.start(
            functools.partial(conv_rows, 1 - pc.c, start, size),
            functools.partial(conv_rows, pc.c, start, size),
        )
    for job in sum_conv:
        job.first()
    forward.third()

    to_child = hot(comes_from, children)
    by_child[...] = dot(to_child, forward.result(), 0, 0)
    total = jnp.zeros(coarse.shape[1:], F32)
    for j in range(OCT):
        child = by_child[pl.ds(j, rows // 4, stride=OCT)].astype(BF16)
        grad = dot(child, cotangent[0], 0, 0)
        for h in range(2):
            down_grad[h, pl.ds(j * width, width)] = grad[:, h * 128 : (h + 1) * 128]
        total += jnp.dot(
            child, down_weight[pl.ds(j * width, width)], preferred_element_type=F32
        )
    sum_down.start(lambda: down_grad[1 - pc.c], lambda: down_grad[pc.c])
    coarse[0] = total.astype(BF16)
    kept = pltpu.make_async_copy(coarse, out_coarse, local_sem.at[3])
    kept.start()

    sum_down.first()
    for job in sums:
        job.second()
    for job in sums:
        job.third()
    for job in sums:
        job.back_second()
    for job in sums:
        job.back_first()
    for i, job in enumerate(sums):
        job.back_core(local_sem.at[i])
    for job in sums:
        job.result()
    kept.wait()
    sender.finish()


def finish(conv_a, conv_x, down, out_conv, out_down, *refs):
    *stored, full_conv, full_down, load_sem, save_sem = refs
    given = (conv_a, conv_x, down)
    half = out_conv.shape[0] // 2
    first_rows = conv_split(half)
    loads = [
        [pltpu.make_async_copy(src.at[h], dst.at[h], load_sem.at[i, h]) for h in range(2)]
        for i, (src, dst) in enumerate(zip(given, stored))
    ]
    for i in range(3):
        for h in range(2):
            loads[i][h].start()
    saves = []
    for i, start, rows in ((0, 0, first_rows), (1, first_rows, half - first_rows)):
        for h in range(2):
            loads[i][h].wait()
            n = stored[i].shape[1]
            chunk = rows // n
            for q in range(n):
                full_conv[pl.ds(h * half + start + q * chunk, chunk)] = stored[i][
                    h, q, pl.ds(0, chunk)
                ].astype(F32)
            at = pl.ds(h * half + start, rows)
            saves.append(
                pltpu.make_async_copy(full_conv.at[at], out_conv.at[at], save_sem.at[i, h])
            )
            saves[-1].start()
    for h in range(2):
        loads[2][h].wait()
        full_down[:, pl.ds(h * 128, 128)] = (
            stored[2][h].reshape(full_down.shape[0], 128).astype(F32)
        )
    saves.append(pltpu.make_async_copy(full_down, out_down, save_sem.at[2, 0]))
    saves[-1].start()
    for save in saves:
        save.wait()


def body(n, nx, *args):
    args = list(args)
    args[1] = jnp.transpose(args[1], (1, 0, 2))
    features, _, _, _, cell_source, conv_weight, _, cotangent = args
    rows, width = features.shape[1:]
    offsets = conv_weight.shape[0]
    cells = cell_source.shape[1]
    cap = cells // (2 * n * n)
    half = offsets * width // 2
    first_rows = conv_split(half)
    exchange = [
        pltpu.VMEM((n, cells // n, width), BF16),
        pltpu.VMEM((n, cells // n, width), BF16),
        pltpu.VMEM((n, 2, cells // n // 2, width), BF16),
        pltpu.VMEM((n, 2, cells // n // 2, width), BF16),
        pltpu.VMEM((2, n, cells // n // 2, width), BF16),
    ]
    sizes = {"a": n, "b": n, "x": nx}
    jobs = [
        (total, *[sizes[name] for name in order])
        for total, order in zip((first_rows, half - first_rows, OCT * width), ORDERS)
    ]
    copies = 2 + 2 * (2 * (n - 1) + 1)
    copies += sum(2 + 2 * (n1 - 1) + 2 * (n2 - 1) + n3 - 1 for _, n1, n2, n3 in jobs)
    hbm = pl.BlockSpec(memory_space=pl.ANY)
    coarse, *parts = pl.pallas_call(
        functools.partial(kernel, n, nx, cap),
        out_shape=[jax.ShapeDtypeStruct(cotangent.shape, BF16)]
        + [
            jax.ShapeDtypeStruct((2, n1, up16(total // n1), 128), BF16) for total, n1, _, _ in jobs
        ],
        in_specs=[hbm] * 8,
        out_specs=[hbm] * 4,
        scratch_shapes=[
            *[
                (pltpu.SMEM if i == 2 else pltpu.VMEM)(arg.shape, arg.dtype)
                for i, arg in enumerate(args)
                if i > 0
            ],
            pltpu.VMEM((rows + 2 * HALO, width), BF16),
            pltpu.VMEM((width, offsets * width), BF16),
            pltpu.VMEM((offsets * width, rows), BF16),
            pltpu.VMEM((cells, width), F32),
            pltpu.VMEM((cells, rows), BF16),
            pltpu.VMEM((cells, cells), BF16),
            pltpu.VMEM((2, OCT * width, 128), F32),
            pltpu.VMEM(cotangent.shape, BF16),
            *exchange,
            *exchange,
            *[ref for job in jobs for ref in Sum.scratch(*job)],
            pltpu.SemaphoreType.DMA((copies,)),
            pltpu.SemaphoreType.DMA((copies,)),
            pltpu.SemaphoreType.DMA((4,)),
            pltpu.SemaphoreType.DMA((8,)),
        ],
        compiler_params=pltpu.CompilerParams(
            collective_id=0, has_side_effects=True, vmem_limit_bytes=64 << 20
        ),
    )(*args)
    grad_conv, grad_down = pl.pallas_call(
        finish,
        out_shape=[
            jax.ShapeDtypeStruct((offsets * width, width), F32),
            jax.ShapeDtypeStruct((OCT * width, 256), F32),
        ],
        in_specs=[hbm] * 3,
        out_specs=[hbm] * 2,
        scratch_shapes=[
            *[pltpu.VMEM(part.shape, BF16) for part in parts],
            pltpu.VMEM((offsets * width, width), F32),
            pltpu.VMEM((OCT * width, 256), F32),
            pltpu.SemaphoreType.DMA((3, 2)),
            pltpu.SemaphoreType.DMA((3, 2)),
        ],
        compiler_params=pltpu.CompilerParams(vmem_limit_bytes=64 << 20),
    )(*parts)
    return (coarse, grad_conv.reshape(offsets, width, width), grad_down)


def solution(mesh):
    n, nx = math.isqrt(mesh.shape["blk"] // 2), mesh.shape["dp"]
    in_specs = (
        P("dp", "blk", None),
        P("dp", None, "blk"),
        P("dp", None),
        P("dp", "blk"),
        P("dp", "blk"),
        P(),
        P(),
        P("dp", "blk", None),
    )
    out_specs = (P("dp", "blk", None), P(), P())
    return jax.shard_map(
        functools.partial(body, n, nx),
        mesh=mesh,
        in_specs=in_specs,
        out_specs=out_specs,
        check_vma=False,
    )
```

time: 88.8 us -> 71.2 us (0.80)
  Pallas kernels: 77.9 us -> 69 us
  local copies, waits for them, and re-layouts: 7.28 us -> 1.38 us
  other arithmetic: 2.45 us -> 0 us
    pallas_call x1, Pallas kernels: 77.9 us -> 66.4 us  [body(): pl.pallas_call(functools.partial(kernel, n, nx, cap), out_shape=[jax.Shap...]
    unnamed x16 -> x1, local copies, waits for them, and re-layouts: 7.18 us -> 1.38 us
    pallas_call x0 -> x1, Pallas kernels: none -> 2.63 us  [body(): pl.pallas_call(finish, out_shape=[jax.ShapeDtypeStruct((offsets * width,...]
    reshape x1 -> x0, other arithmetic: 1.41 us -> none  [body(): conv[:, :, :conv_rows].astype(F32).reshape(offsets, width, width)]
    convert_element_type x1 -> x0, other arithmetic: 1.04 us -> none  [body(): jnp.concatenate([down[0], down[1]], -1).astype(F32)]
where the time goes in v2:
time: 71.2 us; the launch traced here: 71 us
  Pallas kernels  69 us (97%)
  local copies, waits for them, and re-layouts  1.38 us (2%)
    pallas_call x1, Pallas kernels, body(): pl.pallas_call(functools.partial(kernel, n, nx, cap), out_shape=[jax.Shap...  66.4 us
    pallas_call x1, Pallas kernels, body(): pl.pallas_call(finish, out_shape=[jax.ShapeDtypeStruct((offsets * width,...  2.63 us

profile of v2, /device:TPU:1, one launch (start us, length us, event | category | flops | bytes accessed | tf_op | source)
XLA Modules:
  0.0 71.0 jit_solution(11403870694830530116)
XLA Ops:
  0.6 66.4 %shard_map.103 = (bf16[1,64,256]{2,1,0:T(8,128)(2,1)}, bf16[2,8,112,128]{3,2,1,0:T(8,128)(2,1)}, bf16[2,4,224,128]{3,2,1,0:T(8,128)(2,1)}, bf16[2,4,256,128]{3,2,1,0:T(8,128)(2,1)}) custom-call(bf16[1,256,128]{2,1,0:T(8,128)(2,1)} %refs_0_.1, s32[27,1,256]{2,1,0:T(1,128)} %bitcast.2, s32[1,128]{1,0:T(1,128)} %refs_2_.1, s32[1,256]{1,0:T(1,128)} %refs_3_.1, ...), custom_call_target="tpu_custom_call" | custom-call | tf_op jit(solution)/shard_map/pallas_call | solution.py:515
  67.0 2.6 %shard_map.104 = (f32[3456,128]{1,0:T(8,128)}, f32[1024,256]{1,0:T(8,128)}) custom-call(bf16[2,8,112,128]{3,2,1,0:T(8,128)(2,1)} %get-tuple-element.10.conv_a, bf16[2,4,224,128]{3,2,1,0:T(8,128)(2,1)} %get-tuple-element.11.conv_x, bf16[2,4,256,128]{3,2,1,0:T(8,128)(2,1)} %get-tuple-element.12.down), custom_call_target="tpu_custom_call" | custom-call | tf_op jit(solution)/shard_map/pallas_call | solution.py:549
  69.6 1.4 %copy.12 = bf16[1,64,256]{2,1,0:T(8,128)(2,1)} copy(bf16[1,64,256]{2,1,0:T(8,128)(2,1)} %get-tuple-element.18) | data formatting | bytes 65536

commit v3 on v2

--- a/solution.py
+++ b/solution.py
@@ -149,7 +149,7 @@
         return chunk, up16(-(-chunk // n2)), up16(chunk)
 
     @staticmethod
-    def scratch(rows, n1, n2, n3):
+    def scratch(rows, n1, n2, n3, middle):
         _, part, wide = Sum.sizes(rows, n1, n2)
         return [
             pltpu.VMEM((rows, 128), BF16),
@@ -157,9 +157,9 @@
             pltpu.VMEM((rows, 128), F32),
             pltpu.VMEM((n1, wide, 128), BF16),
             pltpu.VMEM((n1, wide, 128), BF16),
-            pltpu.VMEM((n2, part, 128), F32),
-            pltpu.VMEM((n2, part, 128), F32),
-            pltpu.VMEM((n3, part, 128), F32),
+            pltpu.VMEM((n2, part, 128), middle),
+            pltpu.VMEM((n2, part, 128), middle),
+            pltpu.VMEM((n3, part, 128), middle),
             pltpu.VMEM((n2 * part, 128), BF16),
             pltpu.VMEM((n1, wide, 128), BF16),
         ]
@@ -195,7 +195,7 @@
         spare = n * self.part - rows
         if spare:
             total = jnp.concatenate([total, jnp.zeros((spare, 128), F32)], 0)
-        self.s2[...] = total.reshape(self.s2.shape)
+        self.s2[...] = total.reshape(self.s2.shape).astype(self.s2.dtype)
         self.copies = [
             self.sender.start(self.s2.at[lax.rem(me + p, n)], self.r2.at[p], along(p))
             for p in range(1, n)
@@ -204,10 +204,10 @@
     def third(self):
         (n2, me2, _), (n, me, along) = self.axes[1:]
         arrived(self.copies)
-        total = self.s2[me2]
+        total = self.s2[me2].astype(F32)
         for p in range(1, n2):
-            total += self.r2[p]
-        self.s3[me] = total
+            total += self.r2[p].astype(F32)
+        self.s3[me] = total.astype(self.s3.dtype)
         self.copies = [
             self.sender.start(self.s3.at[me], self.s3.at[me], along(p)) for p in range(1, n)
         ]
@@ -215,9 +215,9 @@
     def back_second(self):
         n, me, along = self.axes[1]
         arrived(self.copies)
-        total = self.s3[0]
+        total = self.s3[0].astype(F32)
         for x in range(1, self.axes[2][0]):
-            total += self.s3[x]
+            total += self.s3[x].astype(F32)
         mine = pl.ds(pl.multiple_of(me * self.part, 16), self.part)
         self.g2[mine] = total.astype(BF16)
         self.copies = [
@@ -449,7 +449,7 @@
     sender.finish()
 
 
-def finish(conv_a, conv_x, down, out_conv, out_down, *refs):
+def finish(coarse, conv_a, conv_x, down, out_coarse, out_conv, out_down, *refs):
     *stored, full_conv, full_down, load_sem, save_sem = refs
     given = (conv_a, conv_x, down)
     half = out_conv.shape[0] // 2
@@ -461,7 +461,8 @@
     for i in range(3):
         for h in range(2):
             loads[i][h].start()
-    saves = []
+    saves = [pltpu.make_async_copy(coarse, out_coarse, save_sem.at[2, 1])]
+    saves[0].start()
     for i, start, rows in ((0, 0, first_rows), (1, first_rows, half - first_rows)):
         for h in range(2):
             loads[i][h].wait()
@@ -512,7 +513,7 @@
     copies = 2 + 2 * (2 * (n - 1) + 1)
     copies += sum(2 + 2 * (n1 - 1) + 2 * (n2 - 1) + n3 - 1 for _, n1, n2, n3 in jobs)
     hbm = pl.BlockSpec(memory_space=pl.ANY)
-    coarse, *parts = pl.pallas_call(
+    parts = pl.pallas_call(
         functools.partial(kernel, n, nx, cap),
         out_shape=[jax.ShapeDtypeStruct(cotangent.shape, BF16)]
         + [
@@ -536,7 +537,11 @@
             pltpu.VMEM(cotangent.shape, BF16),
             *exchange,
             *exchange,
-            *[ref for job in jobs for ref in Sum.scratch(*job)],
+            *[
+                ref
+                for job, order in zip(jobs, ORDERS)
+                for ref in Sum.scratch(*job, BF16 if order[0] == "x" else F32)
+            ],
             pltpu.SemaphoreType.DMA((copies,)),
             pltpu.SemaphoreType.DMA((copies,)),
             pltpu.SemaphoreType.DMA((4,)),
@@ -546,16 +551,17 @@
             collective_id=0, has_side_effects=True, vmem_limit_bytes=64 << 20
         ),
     )(*args)
-    grad_conv, grad_down = pl.pallas_call(
+    coarse, grad_conv, grad_down = pl.pallas_call(
         finish,
         out_shape=[
+            jax.ShapeDtypeStruct(cotangent.shape, BF16),
             jax.ShapeDtypeStruct((offsets * width, width), F32),
             jax.ShapeDtypeStruct((OCT * width, 256), F32),
         ],
-        in_specs=[hbm] * 3,
-        out_specs=[hbm] * 2,
+        in_specs=[hbm] * 4,
+        out_specs=[hbm] * 3,
         scratch_shapes=[
-            *[pltpu.VMEM(part.shape, BF16) for part in parts],
+            *[pltpu.VMEM(part.shape, BF16) for part in parts[1:]],
             pltpu.VMEM((offsets * width, width), F32),
             pltpu.VMEM((OCT * width, 256), F32),
             pltpu.SemaphoreType.DMA((3, 2)),

time: 71.2 us -> 67.2 us (0.944)
  Pallas kernels: 69 us -> 66.4 us
  local copies, waits for them, and re-layouts: 1.38 us -> 0 us
    pallas_call x1, Pallas kernels: 66.4 us -> 63.8 us  [body(): pl.pallas_call(functools.partial(kernel, n, nx, cap), out_shape=[jax.Shap...]
    unnamed x1 -> x0, local copies, waits for them, and re-layouts: 1.38 us -> none
where the time goes in v3:
time: 67.2 us; the launch traced here: 67 us
  Pallas kernels  66.4 us (99%)
    pallas_call x1, Pallas kernels, body(): pl.pallas_call(functools.partial(kernel, n, nx, cap), out_shape=[jax.Shap...  63.8 us
    pallas_call x1, Pallas kernels, body(): pl.pallas_call(finish, out_shape=[jax.ShapeDtypeStruct(cotangent.shape, B...  2.63 us

profile of v3, /device:TPU:1, one launch (start us, length us, event | category | flops | bytes accessed | tf_op | source)
XLA Modules:
  0.0 67.0 jit_solution(6481248887510198981)
XLA Ops:
  0.6 63.8 %shard_map.103 = (bf16[1,64,256]{2,1,0:T(8,128)(2,1)}, bf16[2,8,112,128]{3,2,1,0:T(8,128)(2,1)}, bf16[2,4,224,128]{3,2,1,0:T(8,128)(2,1)}, bf16[2,4,256,128]{3,2,1,0:T(8,128)(2,1)}) custom-call(bf16[1,256,128]{2,1,0:T(8,128)(2,1)} %refs_0_.1, s32[27,1,256]{2,1,0:T(1,128)} %bitcast.2, s32[1,128]{1,0:T(1,128)} %refs_2_.1, s32[1,256]{1,0:T(1,128)} %refs_3_.1, ...), custom_call_target="tpu_custom_call" | custom-call | tf_op jit(solution)/shard_map/pallas_call | solution.py:516
  64.4 2.6 %shard_map.104 = (bf16[1,64,256]{2,1,0:T(8,128)(2,1)}, f32[3456,128]{1,0:T(8,128)}, f32[1024,256]{1,0:T(8,128)}) custom-call(bf16[1,64,256]{2,1,0:T(8,128)(2,1)} %get-tuple-element.10.coarse, bf16[2,8,112,128]{3,2,1,0:T(8,128)(2,1)} %get-tuple-element.11.conv_a, bf16[2,4,224,128]{3,2,1,0:T(8,128)(2,1)} %get-tuple-element.12.conv_x, ...), custom_call_target="tpu_custom_call" | custom-call | tf_op jit(solution)/shard_map/pallas_call | solution.py:554

commit v4 on v3

--- a/solution.py
+++ b/solution.py
@@ -81,9 +81,11 @@
         self.all.append(copy)
         return copy
 
-    def finish(self):
-        for copy in self.all:
+    def finish(self, recent=0):
+        old = len(self.all) - recent
+        for copy in self.all[:old]:
             copy.wait_send()
+        self.all = self.all[old:]
 
 
 def arrived(copies):
@@ -92,9 +94,11 @@
 
 
 class Exchange:
-    def __init__(self, place, sender, bufs):
-        self.place, self.sender = place, sender
+    def __init__(self, place, sender, bufs, whole):
+        self.place, self.sender, self.whole = place, sender, whole
         self.send1, self.recv1, self.send2, self.recv2, self.got = bufs
+        if whole:
+            self.recv2 = self.got.at[place.c]
 
     def start(self, rows):
         pc, n = self.place, self.place.n
@@ -124,6 +128,9 @@
     def third(self):
         pc = self.place
         arrived(self.copies)
+        if self.whole:
+            self.copies = [self.sender.start(self.recv2, self.recv2, pc.other_core())]
+            return
         self.copies = [
             self.sender.start(self.recv2.at[:, 1 - pc.c], self.got.at[pc.c], pc.other_core())
         ]
@@ -131,6 +138,9 @@
 
     def result(self):
         arrived(self.copies)
+        if self.whole:
+            rows = [self.got[:, :, core] for core in range(2)]
+            return [flat.reshape(-1, flat.shape[-1]) for flat in rows]
         flat = self.got[...]
         return flat.reshape(-1, flat.shape[-1])
 
@@ -140,8 +150,7 @@
         self.place, self.sender, self.out = place, sender, out
         self.axes = [place.axis(name) for name in order]
         self.rows, self.part, self.wide = self.sizes(rows, *[axis[0] for axis in self.axes[:2]])
-        self.s0, self.r0, self.own, self.s1, self.r1 = bufs[:5]
-        self.s2, self.r2, self.s3, self.g2, self.g1 = bufs[5:]
+        self.own, self.s1, self.r1, self.s2, self.r2, self.s3, self.g2, self.g1 = bufs
 
     @staticmethod
     def sizes(rows, n1, n2):
@@ -152,8 +161,6 @@
     def scratch(rows, n1, n2, n3, middle):
         _, part, wide = Sum.sizes(rows, n1, n2)
         return [
-            pltpu.VMEM((rows, 128), BF16),
-            pltpu.VMEM((rows, 128), BF16),
             pltpu.VMEM((rows, 128), F32),
             pltpu.VMEM((n1, wide, 128), BF16),
             pltpu.VMEM((n1, wide, 128), BF16),
@@ -164,19 +171,10 @@
             pltpu.VMEM((n1, wide, 128), BF16),
         ]
 
-    def start(self, theirs, mine):
-        self.s0[...] = theirs().astype(BF16)
-        self.copies = [self.sender.start(self.s0, self.r0, self.place.other_core())]
-        self.own[...] = mine()
-
     def first(self):
         (n, me, along), rows = self.axes[0], self.rows
-        arrived(self.copies)
         for q in range(n):
-            chunk = pl.ds(q * rows, rows)
-            total = self.own[chunk] + self.r0[chunk].astype(F32)
-            self.own[chunk] = total
-            self.s1[q, pl.ds(0, rows)] = total.astype(BF16)
+            self.s1[q, pl.ds(0, rows)] = self.own[pl.ds(q * rows, rows)].astype(BF16)
             if self.wide > rows:
                 self.s1[q, pl.ds(rows, self.wide - rows)] = jnp.zeros(
                     (self.wide - rows, 128), BF16
@@ -257,9 +255,9 @@
         kernel_map,
         block_counts,
         send_position,
-        cell_source,
         conv_weight,
         down_weight,
+        cell_source,
         cotangent,
         raw,
         weight_t,
@@ -267,8 +265,11 @@
         by_child,
         send_hot,
         swap,
-        down_grad,
         coarse,
+        their_raw,
+        their_map,
+        their_picked,
+        grad_pre,
         *rest,
     ) = refs
     *rest, send_sem, recv_sem, local_sem, load_sem = rest
@@ -288,8 +289,9 @@
     for device in partners:
         pl.semaphore_signal(barrier, inc=1, device_id=device, device_id_type=MESH)
 
-    targets = [raw.at[pl.ds(HALO, rows)], *refs[:7]]
-    sources = [features.at[0], *given[1:]]
+    sources = [features.at[0], *given[1:7], given[7].at[0]]
+    targets = [raw.at[pl.ds(HALO, rows)], kernel_map, block_counts, send_position]
+    targets += [cell_source.at[pc.c], conv_weight, down_weight, cotangent.at[pc.c]]
     loads = [
         pltpu.make_async_copy(src, dst, load_sem.at[i])
         for i, (src, dst) in enumerate(zip(sources, targets))
@@ -310,12 +312,17 @@
             pc.next_block(count - 1, count),
         ),
     ]
-
-    forward = Exchange(pc, sender, rest[0:5])
-    backward = Exchange(pc, sender, rest[5:10])
+    shared = [
+        sender.start(given[4], cell_source.at[pc.c], pc.other_core()),
+        sender.start(given[7].at[0], cotangent.at[pc.c], pc.other_core()),
+    ]
+    shared_map = sender.start(given[1], their_map, pc.other_core())
+
+    forward = Exchange(pc, sender, rest[0:5], True)
+    backward = Exchange(pc, sender, rest[5:10], False)
     first_rows = conv_split(half)
     sums = [
-        Sum(pc, sender, total, order, rest[10 + 10 * i : 20 + 10 * i], outs[i])
+        Sum(pc, sender, total, order, rest[10 + 8 * i : 18 + 8 * i], outs[i])
         for i, (total, order) in enumerate(
             zip((first_rows, half - first_rows, OCT * width), ORDERS)
         )
@@ -338,12 +345,14 @@
     for i in (7, 6, 4):
         loads[i].wait()
     for j in range(OCT):
-        part = dot(cotangent[0], down_weight[pl.ds(j * width, width)], 1, 1)
-        by_child[pl.ds(j, rows // 4, stride=OCT)] = part.astype(BF16).astype(F32)
-    children = cell_source[...]
+        part = dot(cotangent[pc.c], down_weight[pl.ds(j * width, width)], 1, 1)
+        by_child[0, pl.ds(j, rows // 4, stride=OCT)] = part.astype(BF16).astype(F32)
     backward.start(
-        jnp.dot(hot(goes_to, children), by_child[...].astype(BF16), preferred_element_type=F32)
-        .astype(BF16)
+        jnp.dot(
+            hot(goes_to, cell_source[pc.c]),
+            by_child[0].astype(BF16),
+            preferred_element_type=F32,
+        ).astype(BF16)
     )
 
     loads[0].wait()
@@ -361,26 +370,32 @@
     lane = lax.rem(iota((1, rows), 1), 128)
     window = iota((2 * HALO + 128, 128), 0)
     live_t = live_of(pc.blk, iota((1, rows), 1))
-    live = jnp.concatenate(
-        [
-            live_of(pc.blk + count - 1, iota((HALO, width), 0) + rows - HALO),
-            live_of(pc.blk, iota((rows, width), 0)),
-            live_of(pc.blk + 1, iota((HALO, width), 0)),
-        ],
-        0,
-    )
-
-    arrived(halo)
-    table_t = jnp.where(live, raw[...].astype(F32), 0.0).T.astype(BF16)
-    for k in range(offsets):
-        entry = kernel_map[k]
+
+    def table_of(block, ref):
+        live = jnp.concatenate(
+            [
+                live_of(block + count - 1, iota((HALO, width), 0) + rows - HALO),
+                live_of(block, iota((rows, width), 0)),
+                live_of(block + 1, iota((HALO, width), 0)),
+            ],
+            0,
+        )
+        return jnp.where(live, ref[...].astype(F32), 0.0).T.astype(BF16)
+
+    def pick(table_t, entry, k, ref):
         index = jnp.where(entry >= 0, entry + lane, -1)
         for t in range(rows // 128):
             chosen = hot(window, index[:, t * 128 : (t + 1) * 128])
             got = jnp.dot(
                 table_t[:, t * 128 : t * 128 + 128 + 2 * HALO], chosen, preferred_element_type=F32
             )
-            picked[pl.ds(k * width, width), pl.ds(t * 128, 128)] = got.astype(BF16)
+            ref[pl.ds(k * width, width), pl.ds(t * 128, 128)] = got.astype(BF16)
+
+    arrived(halo)
+    shared_raw = sender.start(raw, their_raw, pc.other_core())
+    table_t = table_of(pc.blk, raw)
+    for k in range(offsets):
+        pick(table_t, kernel_map[k], k, picked)
 
     loads[3].wait()
     position = send_position[...]
@@ -395,57 +410,70 @@
     backward.second(swap)
     from_owner = hot(comes_from, position)
     slope = jnp.where(live_t, sig * (1.0 + pre * (1.0 - sig)), 0.0)
+
+    arrived([shared_map, shared_raw])
+    skipped = offsets // 2
+    table_t = table_of(pc.blk + 1 - 2 * pc.c, their_raw)
+    for k in range(offsets - skipped):
+        pick(table_t, their_map[pc.c * skipped + k], k, their_picked)
+
     forward.second(swap)
     backward.third()
     grad_hidden = dot(backward.result(), from_owner, 0, 0)
-    grad_pre = (grad_hidden * slope).astype(BF16)
-
-    def conv_rows(h, start, size):
-        chosen = picked[pl.ds(pl.multiple_of(h * half + start, 16), size)]
-        return dot(chosen, grad_pre, 1, 1)
-
-    for job, start, size in (
+    grad_pre[pc.c] = (grad_hidden * slope).astype(BF16)
+    shared_grad = sender.start(grad_pre.at[pc.c], grad_pre.at[pc.c], pc.other_core())
+    splits = (
         (sum_conv[0], 0, first_rows),
         (sum_conv[1], first_rows, half - first_rows),
-    ):
-        job.start(
-            functools.partial(conv_rows, 1 - pc.c, start, size),
-            functools.partial(conv_rows, pc.c, start, size),
-        )
-    for job in sum_conv:
+    )
+    for job, start, size in splits:
+        mine = picked[pl.ds(pl.multiple_of(pc.c * half + start, 16), size)]
+        job.own[...] = dot(mine, grad_pre[pc.c], 1, 1)
+    arrived([shared_grad])
+    for job, start, size in splits:
+        at = pc.c * (half - skipped * width) + start
+        theirs = their_picked[pl.ds(pl.multiple_of(at, 16), size)]
+        job.own[...] += dot(theirs, grad_pre[1 - pc.c], 1, 1)
         job.first()
     forward.third()
 
-    to_child = hot(comes_from, children)
-    by_child[...] = dot(to_child, forward.result(), 0, 0)
+    arrived(shared)
+    for core, incoming in enumerate(forward.result()):
+        by_child[core] = dot(hot(comes_from, cell_source[core]), incoming, 0, 0)
+    quarter = rows // 4
+    mine = pl.ds(pl.multiple_of(pc.c * 128, 128), 128)
+    wanted = jnp.concatenate([cotangent[core, :, mine] for core in range(2)], 0)
+    for j in range(OCT):
+        child = [by_child[core, pl.ds(j, quarter, stride=OCT)] for core in range(2)]
+        child = jnp.concatenate(child, 0).astype(BF16)
+        sum_down.own[pl.ds(j * width, width)] = dot(child, wanted, 0, 0)
+    sum_down.first()
     total = jnp.zeros(coarse.shape[1:], F32)
     for j in range(OCT):
-        child = by_child[pl.ds(j, rows // 4, stride=OCT)].astype(BF16)
-        grad = dot(child, cotangent[0], 0, 0)
-        for h in range(2):
-            down_grad[h, pl.ds(j * width, width)] = grad[:, h * 128 : (h + 1) * 128]
+        child = by_child[pc.c, pl.ds(j, quarter, stride=OCT)].astype(BF16)
         total += jnp.dot(
             child, down_weight[pl.ds(j * width, width)], preferred_element_type=F32
         )
-    sum_down.start(lambda: down_grad[1 - pc.c], lambda: down_grad[pc.c])
     coarse[0] = total.astype(BF16)
     kept = pltpu.make_async_copy(coarse, out_coarse, local_sem.at[3])
     kept.start()
 
-    sum_down.first()
     for job in sums:
         job.second()
     for job in sums:
         job.third()
     for job in sums:
         job.back_second()
+    sent = len(sender.all)
     for job in sums:
         job.back_first()
+    sender.finish(len(sender.all) - sent)
     for i, job in enumerate(sums):
         job.back_core(local_sem.at[i])
+    kept.wait()
+    sender.finish(len(sums))
     for job in sums:
         job.result()
-    kept.wait()
     sender.finish()
 
 
@@ -503,15 +531,16 @@
         pltpu.VMEM((n, cells // n, width), BF16),
         pltpu.VMEM((n, 2, cells // n // 2, width), BF16),
         pltpu.VMEM((n, 2, cells // n // 2, width), BF16),
-        pltpu.VMEM((2, n, cells // n // 2, width), BF16),
     ]
+    one = pltpu.VMEM((2, n, cells // n // 2, width), BF16)
+    both = pltpu.VMEM((2, n, 2, cells // n // 2, width), BF16)
     sizes = {"a": n, "b": n, "x": nx}
     jobs = [
         (total, *[sizes[name] for name in order])
         for total, order in zip((first_rows, half - first_rows, OCT * width), ORDERS)
     ]
-    copies = 2 + 2 * (2 * (n - 1) + 1)
-    copies += sum(2 + 2 * (n1 - 1) + 2 * (n2 - 1) + n3 - 1 for _, n1, n2, n3 in jobs)
+    copies = 7 + 2 * (2 * (n - 1) + 1)
+    copies += sum(1 + 2 * (n1 - 1) + 2 * (n2 - 1) + n3 - 1 for _, n1, n2, n3 in jobs)
     hbm = pl.BlockSpec(memory_space=pl.ANY)
     parts = pl.pallas_call(
         functools.partial(kernel, n, nx, cap),
@@ -523,20 +552,26 @@
         out_specs=[hbm] * 4,
         scratch_shapes=[
             *[
-                (pltpu.SMEM if i == 2 else pltpu.VMEM)(arg.shape, arg.dtype)
-                for i, arg in enumerate(args)
-                if i > 0
+                (pltpu.SMEM if i == 2 else pltpu.VMEM)(args[i].shape, args[i].dtype)
+                for i in (1, 2, 3, 5, 6)
             ],
+            pltpu.VMEM((2, 1, cells), jnp.int32),
+            pltpu.VMEM((2, *cotangent.shape[1:]), BF16),
             pltpu.VMEM((rows + 2 * HALO, width), BF16),
             pltpu.VMEM((width, offsets * width), BF16),
             pltpu.VMEM((offsets * width, rows), BF16),
-            pltpu.VMEM((cells, width), F32),
+            pltpu.VMEM((2, cells, width), F32),
             pltpu.VMEM((cells, rows), BF16),
             pltpu.VMEM((cells, cells), BF16),
-            pltpu.VMEM((2, OCT * width, 128), F32),
             pltpu.VMEM(cotangent.shape, BF16),
+            pltpu.VMEM((rows + 2 * HALO, width), BF16),
+            pltpu.VMEM(args[1].shape, jnp.int32),
+            pltpu.VMEM(((offsets - offsets // 2) * width, rows), BF16),
+            pltpu.VMEM((2, width, rows), BF16),
             *exchange,
+            both,
             *exchange,
+            one,
             *[
                 ref
                 for job, order in zip(jobs, ORDERS)

time: 67.2 us -> 66.3 us (0.987)
  Pallas kernels: 66.4 us -> 65.5 us
    pallas_call x1, Pallas kernels: 63.8 us -> 62.8 us  [body(): pl.pallas_call(functools.partial(kernel, n, nx, cap), out_shape=[jax.Shap...]
where the time goes in v4:
time: 66.3 us; the launch traced here: 66.1 us
  Pallas kernels  65.5 us (99%)
    pallas_call x1, Pallas kernels, body(): pl.pallas_call(functools.partial(kernel, n, nx, cap), out_shape=[jax.Shap...  62.8 us
    pallas_call x1, Pallas kernels, body(): pl.pallas_call(finish, out_shape=[jax.ShapeDtypeStruct(cotangent.shape, B...  2.63 us

profile of v4, /device:TPU:1, one launch (start us, length us, event | category | flops | bytes accessed | tf_op | source)
XLA Modules:
  0.0 66.1 jit_solution(12436946866980084717)
XLA Ops:
  0.6 62.8 %shard_map.103 = (bf16[1,64,256]{2,1,0:T(8,128)(2,1)}, bf16[2,8,112,128]{3,2,1,0:T(8,128)(2,1)}, bf16[2,4,224,128]{3,2,1,0:T(8,128)(2,1)}, bf16[2,4,256,128]{3,2,1,0:T(8,128)(2,1)}) custom-call(bf16[1,256,128]{2,1,0:T(8,128)(2,1)} %refs_0_.1, s32[27,1,256]{2,1,0:T(1,128)} %bitcast.2, s32[1,128]{1,0:T(1,128)} %refs_2_.1, s32[1,256]{1,0:T(1,128)} %refs_3_.1, ...), custom_call_target="tpu_custom_call" | custom-call | tf_op jit(solution)/shard_map/pallas_call | solution.py:545
  63.5 2.6 %shard_map.104 = (bf16[1,64,256]{2,1,0:T(8,128)(2,1)}, f32[3456,128]{1,0:T(8,128)}, f32[1024,256]{1,0:T(8,128)}) custom-call(bf16[1,64,256]{2,1,0:T(8,128)(2,1)} %get-tuple-element.10.coarse, bf16[2,8,112,128]{3,2,1,0:T(8,128)(2,1)} %get-tuple-element.11.conv_a, bf16[2,4,224,128]{3,2,1,0:T(8,128)(2,1)} %get-tuple-element.12.conv_x, ...), custom_call_target="tpu_custom_call" | custom-call | tf_op jit(solution)/shard_map/pallas_call | solution.py:589

commit v5 on v4

--- a/solution.py
+++ b/solution.py
@@ -25,6 +25,10 @@
 
 def up16(rows):
     return -(-rows // 16) * 16
+
+
+def far_first(n):
+    return sorted(range(1, n), key=lambda p: -min(p, n - p))
 
 
 class Place:
@@ -107,7 +111,7 @@
             self.sender.start(
                 self.send1.at[lax.rem(pc.a + p, n)], self.recv1.at[pc.a], pc.along_a(p)
             )
-            for p in range(1, n)
+            for p in far_first(n)
         ]
         self.recv1[pc.a] = self.send1[pc.a]
 
@@ -121,7 +125,7 @@
             self.sender.start(
                 self.send2.at[lax.rem(pc.b + p, n)], self.recv2.at[pc.b], pc.along_b(p)
             )
-            for p in range(1, n)
+            for p in far_first(n)
         ]
         self.recv2[pc.b] = self.send2[pc.b]
 
@@ -181,7 +185,7 @@
                 )
         self.copies = [
             self.sender.start(self.s1.at[lax.rem(me + p, n)], self.r1.at[p], along(p))
-            for p in range(1, n)
+            for p in far_first(n)
         ]
 
     def second(self):
@@ -196,7 +200,7 @@
         self.s2[...] = total.reshape(self.s2.shape).astype(self.s2.dtype)
         self.copies = [
             self.sender.start(self.s2.at[lax.rem(me + p, n)], self.r2.at[p], along(p))
-            for p in range(1, n)
+            for p in far_first(n)
         ]
 
     def third(self):
@@ -207,7 +211,7 @@
             total += self.r2[p].astype(F32)
         self.s3[me] = total.astype(self.s3.dtype)
         self.copies = [
-            self.sender.start(self.s3.at[me], self.s3.at[me], along(p)) for p in range(1, n)
+            self.sender.start(self.s3.at[me], self.s3.at[me], along(p)) for p in far_first(n)
         ]
 
     def back_second(self):
@@ -219,7 +223,7 @@
         mine = pl.ds(pl.multiple_of(me * self.part, 16), self.part)
         self.g2[mine] = total.astype(BF16)
         self.copies = [
-            self.sender.start(self.g2.at[mine], self.g2.at[mine], along(p)) for p in range(1, n)
+            self.sender.start(self.g2.at[mine], self.g2.at[mine], along(p)) for p in far_first(n)
         ]
 
     def back_first(self):
@@ -227,7 +231,7 @@
         arrived(self.copies)
         self.g1[me] = self.g2[pl.ds(0, self.wide)]
         self.copies = [
-            self.sender.start(self.g1.at[me], self.g1.at[me], along(p)) for p in range(1, n)
+            self.sender.start(self.g1.at[me], self.g1.at[me], along(p)) for p in far_first(n)
         ]
 
     def back_core(self, sem):

time: 66.3 us -> 63.3 us (0.955)
  Pallas kernels: 65.5 us -> 62.5 us
    pallas_call x1, Pallas kernels: 62.8 us -> 59.9 us  [body(): pl.pallas_call(functools.partial(kernel, n, nx, cap), out_shape=[jax.Shap...]
where the time goes in v5:
time: 63.3 us; the launch traced here: 63.2 us
  Pallas kernels  62.5 us (99%)
  between operations  0.64 us (1%)
    pallas_call x1, Pallas kernels, body(): pl.pallas_call(functools.partial(kernel, n, nx, cap), out_shape=[jax.Shap...  59.9 us
    pallas_call x1, Pallas kernels, body(): pl.pallas_call(finish, out_shape=[jax.ShapeDtypeStruct(cotangent.shape, B...  2.63 us

profile of v5, /device:TPU:1, one launch (start us, length us, event | category | flops | bytes accessed | tf_op | source)
XLA Modules:
  0.0 63.2 jit_solution(171588926597256678)
XLA Ops:
  0.6 59.9 %shard_map.103 = (bf16[1,64,256]{2,1,0:T(8,128)(2,1)}, bf16[2,8,112,128]{3,2,1,0:T(8,128)(2,1)}, bf16[2,4,224,128]{3,2,1,0:T(8,128)(2,1)}, bf16[2,4,256,128]{3,2,1,0:T(8,128)(2,1)}) custom-call(bf16[1,256,128]{2,1,0:T(8,128)(2,1)} %refs_0_.1, s32[27,1,256]{2,1,0:T(1,128)} %bitcast.2, s32[1,128]{1,0:T(1,128)} %refs_2_.1, s32[1,256]{1,0:T(1,128)} %refs_3_.1, ...), custom_call_target="tpu_custom_call" | custom-call | tf_op jit(solution)/shard_map/pallas_call | solution.py:549
  60.5 2.6 %shard_map.104 = (bf16[1,64,256]{2,1,0:T(8,128)(2,1)}, f32[3456,128]{1,0:T(8,128)}, f32[1024,256]{1,0:T(8,128)}) custom-call(bf16[1,64,256]{2,1,0:T(8,128)(2,1)} %get-tuple-element.10.coarse, bf16[2,8,112,128]{3,2,1,0:T(8,128)(2,1)} %get-tuple-element.11.conv_a, bf16[2,4,224,128]{3,2,1,0:T(8,128)(2,1)} %get-tuple-element.12.conv_x, ...), custom_call_target="tpu_custom_call" | custom-call | tf_op jit(solution)/shard_map/pallas_call | solution.py:593

commit v6 on v5

--- a/solution.py
+++ b/solution.py
@@ -177,16 +177,16 @@
 
     def first(self):
         (n, me, along), rows = self.axes[0], self.rows
-        for q in range(n):
-            self.s1[q, pl.ds(0, rows)] = self.own[pl.ds(q * rows, rows)].astype(BF16)
+        self.copies = []
+        for p in far_first(n):
+            q = lax.rem(me + p, n)
+            chunk = self.own[pl.ds(pl.multiple_of(q * rows, 8), rows)]
+            self.s1[q, pl.ds(0, rows)] = chunk.astype(BF16)
             if self.wide > rows:
                 self.s1[q, pl.ds(rows, self.wide - rows)] = jnp.zeros(
                     (self.wide - rows, 128), BF16
                 )
-        self.copies = [
-            self.sender.start(self.s1.at[lax.rem(me + p, n)], self.r1.at[p], along(p))
-            for p in far_first(n)
-        ]
+            self.copies.append(self.sender.start(self.s1.at[q], self.r1.at[p], along(p)))
 
     def second(self):
         (n1, me1, _), (n, me, along), rows = self.axes[0], self.axes[1], self.rows

time: 63.3 us -> 63.3 us (level)
  no operation moved by 1% of the time
where the time goes in v6:
time: 63.3 us; the launch traced here: 63.1 us
  Pallas kernels  62.5 us (99%)
  between operations  0.64 us (1%)
    pallas_call x1, Pallas kernels, body(): pl.pallas_call(functools.partial(kernel, n, nx, cap), out_shape=[jax.Shap...  59.9 us
    pallas_call x1, Pallas kernels, body(): pl.pallas_call(finish, out_shape=[jax.ShapeDtypeStruct(cotangent.shape, B...  2.63 us

profile of v6, /device:TPU:1, one launch (start us, length us, event | category | flops | bytes accessed | tf_op | source)
XLA Modules:
  0.0 63.1 jit_solution(4416263615132314574)
XLA Ops:
  0.6 59.9 %shard_map.103 = (bf16[1,64,256]{2,1,0:T(8,128)(2,1)}, bf16[2,8,112,128]{3,2,1,0:T(8,128)(2,1)}, bf16[2,4,224,128]{3,2,1,0:T(8,128)(2,1)}, bf16[2,4,256,128]{3,2,1,0:T(8,128)(2,1)}) custom-call(bf16[1,256,128]{2,1,0:T(8,128)(2,1)} %refs_0_.1, s32[27,1,256]{2,1,0:T(1,128)} %bitcast.2, s32[1,128]{1,0:T(1,128)} %refs_2_.1, s32[1,256]{1,0:T(1,128)} %refs_3_.1, ...), custom_call_target="tpu_custom_call" | custom-call | tf_op jit(solution)/shard_map/pallas_call | solution.py:549
  60.5 2.6 %shard_map.104 = (bf16[1,64,256]{2,1,0:T(8,128)(2,1)}, f32[3456,128]{1,0:T(8,128)}, f32[1024,256]{1,0:T(8,128)}) custom-call(bf16[1,64,256]{2,1,0:T(8,128)(2,1)} %get-tuple-element.10.coarse, bf16[2,8,112,128]{3,2,1,0:T(8,128)(2,1)} %get-tuple-element.11.conv_a, bf16[2,4,224,128]{3,2,1,0:T(8,128)(2,1)} %get-tuple-element.12.conv_x, ...), custom_call_target="tpu_custom_call" | custom-call | tf_op jit(solution)/shard_map/pallas_call | solution.py:593
